TPU v7x, 512 devices: a whole 4x4x16 slice. The times are simulated.
512 devices in a mesh: dp: 8 (over y_hi, x), expert: 64 (over z, y_lo, core).
Axes of the slice: x: 4, y: 4 (y_hi: 2, y_lo: 2; y = y_hi * 2 + y_lo), z: 16, core: 2. Of those that a mesh axis runs over, the one named last changes fastest.
Arguments:
- tokens: bfloat16 [8192, 4096], P('expert', 'dp'), may hold values from -6 to 6
- expert_ids: int32 [8192, 8], P('expert'), may hold values from 0 to 63, all different within a row; in each aligned block of 128 rows (0 to 127, 128 to 255, ...) at most 19 rows name the same one
- route_weight: float32 [8192, 8], P('expert'), may hold values from 0.1 to 1
- placement: int32 [64], replicated, may hold values from 0 to 63, each once
- swap_flag: int32 [32], replicated, may hold values 0 or 1
- gate_up: bfloat16 [64, 2, 768, 4096], P('expert', None, 'dp'), may hold values from -0.09375 to 0.09375
- down_weight: bfloat16 [64, 768, 4096], P('expert', None, 'dp'), may hold values from -0.21875 to 0.21875
Outputs:
- moe_out: bfloat16 [8192, 4096], P('expert', 'dp')
- column_load: float32 [64], replicated
- slot_gate_up: bfloat16 [64, 2, 768, 4096], P('expert', None, 'dp')
- slot_down: bfloat16 [64, 768, 4096], P('expert', None, 'dp')
Inputs may be any that keep to these rules, and one draw needn't show every extreme that they name: `expert_ids`: within the rows of one device (aligned blocks of 128 tokens) no expert is chosen more than 19 times, and some expert is chosen exactly 19 times; a token's 8 experts differ. A permutation: expert e's weights are in slot placement[e]. swap_flag[p] = 1 means slots p and p + 32 exchange owners.
All inputs are finite; a program needn't handle non-finite values.
Results may differ from a plain program's by a relative error of at most 0.0057.
Values may be sent and summed in bfloat16 or wider, within the bound.
A program may use at most 128 MiB of HBM per device.

v0:
```python
import jax
import jax.numpy as jnp
from jax import lax
from jax.sharding import PartitionSpec as P


def from_behind(value, axis, steps):
    count = lax.axis_size(axis)
    pairs = [(source, (source + steps) % count) for source in range(count)]
    return lax.ppermute(value, axis, pairs)


def swapped_blocks(gate_up, down_weight, swap_flag, pair_index, half):
    incoming_pair = from_behind(gate_up, "expert", half)
    incoming_down = from_behind(down_weight, "expert", half)
    own_column = lax.axis_index("expert")
    own_flag = jnp.sum(jnp.where(pair_index == own_column % half, swap_flag, 0))
    pair_after = jnp.where(own_flag == 1, incoming_pair, gate_up)
    down_after = jnp.where(own_flag == 1, incoming_down, down_weight)
    return (pair_after, down_after)


def body(tokens, expert_ids, route_weight, placement, swap_flag, gate_up, down_weight):
    ncol = lax.axis_size("expert")
    half = ncol // 2
    rows_here, feat_here = tokens.shape
    topk = expert_ids.shape[1]
    hid_here = gate_up.shape[2]
    width = gate_up.shape[3]
    capacity = max(4, rows_here * topk * 17 // (16 * ncol) + 2)
    experts_all = placement.shape[0]
    pair_index = jnp.arange(half, dtype=jnp.int32)
    hits = placement[:, None] % half == pair_index[None, :]
    flag_of = jnp.sum(jnp.where(hits, swap_flag[None, :], 0), axis=1)
    moved = (placement + half * flag_of) % ncol
    picks = expert_ids.reshape(-1)[:, None] == jnp.arange(experts_all, dtype=jnp.int32)[None, :]
    moved_dest = jnp.sum(jnp.where(picks, moved[None, :], 0), axis=1)
    columns = jnp.arange(ncol, dtype=jnp.int32)
    local_counts = jnp.sum((moved_dest[:, None] == columns[None, :]).astype(jnp.float32), axis=0)
    totals = lax.psum(local_counts, "expert")
    column_load = totals / jnp.float32(rows_here * topk)
    slot_gate_up, slot_down = swapped_blocks(gate_up, down_weight, swap_flag, pair_index, half)
    col_hits = moved_dest[:, None] == columns[None, :]
    order = jnp.cumsum(col_hits.astype(jnp.int32), axis=0) - 1
    position = jnp.sum(jnp.where(col_hits, order, 0), axis=1)
    slot_index = moved_dest * capacity + position
    w_pair = slot_gate_up.reshape(2 * hid_here, width)
    w_down = slot_down.reshape(slot_down.shape[1], feat_here)
    contract = (((1,), (1,)), ((), ()))
    whole = lax.all_gather(tokens, "dp", axis=1, tiled=True)
    repeated = jnp.repeat(whole, topk, axis=0)
    buffer = jnp.zeros((ncol * capacity, width), jnp.bfloat16).at[slot_index].set(repeated)
    buffer = buffer.reshape(ncol, capacity, width)
    received = lax.all_to_all(buffer, "expert", split_axis=0, concat_axis=0, tiled=True)
    blocks, count, wide = received.shape
    rows = received.reshape(blocks * count, wide)
    projected = lax.dot_general(rows, w_pair, contract, preferred_element_type=jnp.float32)
    hidden = (jax.nn.silu(projected[:, :hid_here]) * projected[:, hid_here:]).astype(jnp.bfloat16)
    mixed = jnp.dot(
        lax.all_gather(hidden, "dp", axis=1, tiled=True), w_down, preferred_element_type=jnp.float32
    )
    result = mixed.astype(jnp.bfloat16).reshape(blocks, count, feat_here)
    returned = lax.all_to_all(result, "expert", split_axis=0, concat_axis=0, tiled=True)
    flat_back = returned.reshape(ncol * capacity, feat_here)
    gathered = flat_back[slot_index].astype(jnp.float32).reshape(rows_here, topk, feat_here)
    moe_out = jnp.sum(gathered * route_weight[:, :, None], axis=1).astype(jnp.bfloat16)
    return (moe_out, column_load, slot_gate_up, slot_down)


def solution(mesh):
    return jax.shard_map(
        body,
        mesh=mesh,
        in_specs=(
            P("expert", "dp"),
            P("expert", None),
            P("expert", None),
            P(),
            P(),
            P("expert", None, "dp", None),
            P("expert", None, "dp"),
        ),
        out_specs=(P("expert", "dp"), P(), P("expert", None, "dp", None), P("expert", None, "dp")),
        check_vma=False,
    )
```

profile of v0, /device:TPU:6, one launch (start us, length us, event | category | flops | bytes accessed | tf_op | source)
XLA Modules:
  0.0 1084.8 jit_solution(5621676649400617664)
XLA Ops:
  7.2 0.7 all-gather.3.cloned.1.call-update
  7.9 0.8 copy.16
  8.8 0.7 and_select_fusion.1
  9.4 0.7 select_reduce_fusion.1
  11.0 18.0 %reduce-window.6 = s32[64,8,128]{2,1,0:T(8,128)S(1)} reduce-window(s32[64,8,128]{2,1,0:T(8,128)S(1)} %fusion.9, s32[]{:T(128)} %constant.51.clone.1), window={size=1x1x128 pad=0_0x0_0x127_0}, to_apply=%region_2.3 | reduce-window | flops 8323072 | bytes 524292 | tf_op jit(solution)/shard_map/reduce-window
  29.6 49.2 %all-gather.3.cloned.1.call-done = bf16[128,4096]{1,0:T(8,128)(2,1)} async-done(((bf16[128,512]{1,0:T(8,128)(2,1)}), bf16[128,4096]{1,0:T(8,128)(2,1)}) %all-gather.3.cloned.1.call-update) | async-done | bytes 1048592 | tf_op jit(solution)/shard_map/all_gather | solution.py:50
  78.8 17.4 %scatter_custom_fusion = bf16[1216,4096]{1,0:T(8,128)(2,1)} fusion(s32[1024]{0:T(1024)S(1)} %bitcast.35, bf16[]{:T(256)} %constant.50.clone.1, bf16[128,4096]{1,0:T(8,128)(2,1)} %all-gather.3.cloned.1.call-done), kind=kCustom, calls=%fused_computation.2 | custom fusion | bytes 11010050 | tf_op jit(solution)/shard_map/scatter | solution.py:52
  96.2 11.4 %reshape.90 = bf16[64,19,4096]{2,1,0:T(8,128)(2,1)} reshape(bf16[1216,4096]{1,0:T(8,128)(2,1)} %scatter_custom_fusion) | data formatting | bytes 19922944 | tf_op jit(solution)/shard_map/reshape | solution.py:53
  107.6 13.8 %all-to-all-start = ((bf16[64,19,4096]{2,1,0:T(8,128)(2,1)}), bf16[64,19,4096]{2,1,0:T(8,128)(2,1)}, u32[]{:S(2)}, u32[]{:S(2)}) async-start(bf16[64,19,4096]{2,1,0:T(8,128)(2,1)} %reshape.90), calls=%async_computation | async-start | bytes 25165824 | tf_op jit(solution)/shard_map/all_to_all | solution.py:54
  121.5 12.2 %collective-permute-start = (bf16[1,2,96,4096]{3,2,1,0:T(8,128)(2,1)S(1)}, bf16[1,2,96,4096]{3,2,1,0:T(8,128)(2,1)}, u32[]{:S(2)}, u32[]{:S(2)}) collective-permute-start(bf16[1,2,96,4096]{3,2,1,0:T(8,128)(2,1)S(1)} %copy-done), channel_id=1, source_target_pairs={{0,32},{1,33},{2,34},{3,35},{4,36},{5,37},{6,38},{7,39},{8,40},{9,... | collective-permute-start | bytes 4718600 | tf_op jit(solution)/shard_map/ppermute | solution.py:10
  135.0 671.5 %collective-permute-done = bf16[1,2,96,4096]{3,2,1,0:T(8,128)(2,1)} collective-permute-done((bf16[1,2,96,4096]{3,2,1,0:T(8,128)(2,1)S(1)}, bf16[1,2,96,4096]{3,2,1,0:T(8,128)(2,1)}, u32[]{:S(2)}, u32[]{:S(2)}) %collective-permute-start) | collective-permute-done | bytes 1572896 | tf_op jit(solution)/shard_map/ppermute | solution.py:10
  806.5 1.6 broadcast_select_fusion
  808.1 12.3 %reshape.91 = bf16[1216,4096]{1,0:T(8,128)(2,1)} reshape(bf16[64,19,4096]{2,1,0:T(8,128)(2,1)} %all-to-all-done) | data formatting | bytes 19922944 | tf_op jit(solution)/shard_map/reshape | solution.py:56
  820.4 7.1 fusion.13
  827.5 0.8 fusion.6
  828.4 1.9 collective-permute-start.1
  830.4 27.8 %collective-permute-done.1 = bf16[1,768,512]{2,1,0:T(8,128)(2,1)S(1)} collective-permute-done((bf16[1,768,512]{2,1,0:T(8,128)(2,1)S(1)}, bf16[1,768,512]{2,1,0:T(8,128)(2,1)S(1)}, u32[]{:S(2)}, u32[]{:S(2)}) %collective-permute-start.1) | collective-permute-done | bytes 786464 | tf_op jit(solution)/shard_map/ppermute | solution.py:10
  858.3 29.5 %all-gather.5.cloned.1.call-done = bf16[1216,768]{0,1:T(8,128)(2,1)} async-done(((bf16[1216,96]{0,1:T(8,128)(2,1)}), bf16[1216,768]{0,1:T(8,128)(2,1)}) %all-gather.5.cloned.1.call-update) | async-done | bytes 1867792 | tf_op jit(solution)/shard_map/all_gather | solution.py:60
  887.7 2.7 convolution_convert_fusion
  890.4 1.4 reshape.94
  891.8 13.4 %all-to-all-start.1 = ((bf16[64,19,512]{2,1,0:T(8,128)(2,1)}), bf16[64,19,512]{2,1,0:T(8,128)(2,1)S(1)}, u32[]{:S(2)}, u32[]{:S(2)}) async-start(bf16[64,19,512]{2,1,0:T(8,128)(2,1)} %reshape.94), calls=%async_computation.1 | async-start | bytes 3145728 | tf_op jit(solution)/shard_map/all_to_all | solution.py:63
  905.4 166.2 %psum.7 = f32[64]{0:T(128)S(1)} all-reduce(f32[64]{0:T(128)S(1)} %convert_reduce_fusion), channel_id=1, replica_groups=mesh['dp'=8,'expert'=64] {'expert'}, use_global_device_ids=true, to_apply=%region_9.10 | all-reduce | flops 64 | bytes 512 | tf_op jit(solution)/shard_map/psum | solution.py:40
  1072.7 4.0 gather_fusion
  1076.6 1.3 fusion.4
  (37 shorter events, 3.5 us)
Async XLA Ops:
  7.2 71.6 %all-gather.3.cloned.1.call-start = ((), (), s32[]{:S(2)}) async-start(), calls=%async_computation.2 | async-start | bytes 1179648 | tf_op jit(solution)/shard_map/all_gather | solution.py:50
  107.6 13.8 %copy-start = (bf16[1,2,96,4096]{3,2,1,0:T(8,128)(2,1)S(1)}, bf16[1,2,96,4096]{3,2,1,0:T(8,128)(2,1)}, u32[]{:S(2)}) copy-start(bf16[1,2,96,4096]{3,2,1,0:T(8,128)(2,1)} %param.12) | copy-start | bytes 4718596
  107.6 26.1 %copy-start.5 = (s32[32]{0:T(128)S(1)}, s32[32]{0:T(128)}, u32[]{:S(2)}) copy-start(s32[32]{0:T(128)} %param.11) | copy-start | bytes 388
  107.6 700.5 %all-to-all-start = ((bf16[64,19,4096]{2,1,0:T(8,128)(2,1)}), bf16[64,19,4096]{2,1,0:T(8,128)(2,1)}, u32[]{:S(2)}, u32[]{:S(2)}) async-start(bf16[64,19,4096]{2,1,0:T(8,128)(2,1)} %reshape.90), calls=%async_computation | async-start | bytes 25165824 | tf_op jit(solution)/shard_map/all_to_all | solution.py:54
  121.4 766.3 %all-gather.5.cloned.1.call-start = ((), (), s32[]{:S(2)}) async-start(), calls=%async_computation.3 | async-start | bytes 2211840 | tf_op jit(solution)/shard_map/all_gather | solution.py:60
  121.5 685.0 %collective-permute-start = (bf16[1,2,96,4096]{3,2,1,0:T(8,128)(2,1)S(1)}, bf16[1,2,96,4096]{3,2,1,0:T(8,128)(2,1)}, u32[]{:S(2)}, u32[]{:S(2)}) collective-permute-start(bf16[1,2,96,4096]{3,2,1,0:T(8,128)(2,1)S(1)} %copy-done), channel_id=1, source_target_pairs={{0,32},{1,33},{2,34},{3,35},{4,36},{5,37},{6,38},{7,39},{8,40},{9,... | collective-permute-start | bytes 4718600 | tf_op jit(solution)/shard_map/ppermute | solution.py:10
  808.1 12.3 %copy-start.1 = (bf16[1,2,96,4096]{3,2,1,0:T(8,128)(2,1)}, bf16[1,2,96,4096]{3,2,1,0:T(8,128)(2,1)S(1)}, u32[]{:S(2)}) copy-start(bf16[1,2,96,4096]{3,2,1,0:T(8,128)(2,1)S(1)} %broadcast_select_fusion) | copy-start | bytes 4718596
  820.4 8.0 copy-start.2
  828.4 29.7 %collective-permute-start.1 = (bf16[1,768,512]{2,1,0:T(8,128)(2,1)S(1)}, bf16[1,768,512]{2,1,0:T(8,128)(2,1)S(1)}, u32[]{:S(2)}, u32[]{:S(2)}) collective-permute-start(bf16[1,768,512]{2,1,0:T(8,128)(2,1)S(1)} %copy-done.2), channel_id=1, source_target_pairs={{0,32},{1,33},{2,34},{3,35},{4,36},{5,37},{6,38},{7,39},{8,40},{9,... | collective-permute-start | bytes 2359304 | tf_op jit(solution)/shard_map/ppermute | solution.py:10
  858.2 32.2 %copy-start.3 = (bf16[1,768,512]{2,1,0:T(8,128)(2,1)}, bf16[1,768,512]{2,1,0:T(8,128)(2,1)S(1)}, u32[]{:S(2)}) copy-start(bf16[1,768,512]{2,1,0:T(8,128)(2,1)S(1)} %broadcast_select_fusion.1) | copy-start | bytes 2359300
  891.8 13.4 %copy-start.4 = (f32[128,8]{0,1:T(8,128)S(1)}, f32[128,8]{0,1:T(8,128)}, u32[]{:S(2)}) copy-start(f32[128,8]{0,1:T(8,128)} %param.9) | copy-start | bytes 12292
  891.8 180.4 %all-to-all-start.1 = ((bf16[64,19,512]{2,1,0:T(8,128)(2,1)}), bf16[64,19,512]{2,1,0:T(8,128)(2,1)S(1)}, u32[]{:S(2)}, u32[]{:S(2)}) async-start(bf16[64,19,512]{2,1,0:T(8,128)(2,1)} %reshape.94), calls=%async_computation.1 | async-start | bytes 3145728 | tf_op jit(solution)/shard_map/all_to_all | solution.py:63
Sparse Core Ops, SparseCore 0:
  11.1 67.6 all-gather.2
  828.5 59.1 all-gather.4
where the time goes:
time: 1090 us; the launch traced here: 1080 us
  waiting for transfers between devices  779 us (71%)
  blocking collectives  166 us (15%)
  local copies, waits for them, and re-layouts  48.3 us (4%)
  starting transfers between devices  41.3 us (4%)
  other arithmetic  25.6 us (2%)
  between operations  14.9 us (1%)
    ppermute x2, waiting for transfers between devices, from_behind(): return lax.ppermute(value, axis, pairs)  699 us
    psum x1, blocking collectives, body(): totals = lax.psum(local_counts, 'expert')  166 us
    all_gather x1, waiting for transfers between devices, body(): whole = lax.all_gather(tokens, 'dp', axis=1, tiled=True)  49.2 us
    all_gather x1, waiting for transfers between devices, body(): lax.all_gather(hidden, 'dp', axis=1, tiled=True)  29.5 us
  transfers between devices with their start and end apart: 6, of which 4 were waited for; matrix products, arithmetic and copies ran while one was open for 2% of the time, Pallas kernels for 0%

commit v1 on v0

v1 whole, which is shorter than its diff:
```python
import jax
import jax.numpy as jnp
from jax import lax
from jax.experimental import pallas as pl
from jax.experimental.pallas import tpu as pltpu
from jax.sharding import PartitionSpec as P

MESH = pl.DeviceIdType.MESH
BF = jnp.bfloat16
F32 = jnp.float32
NT = (((1,), (1,)), ((), ()))
TN = (((0,), (0,)), ((), ()))

NE = 64
TOK = 128
FEAT = 512
MAIN, EXT = 16, 4
WIDE = FEAT + 128
UNITS = 96
ROWS = NE * (MAIN + EXT)
TILE = 256


def iota(shape, axis):
    return lax.broadcasted_iota(jnp.int32, shape, axis)


def flag(cond, dtype=BF):
    return jnp.where(cond, 1.0, 0.0).astype(dtype)


def shuffle_matrix():
    row, col = iota((128, 128), 0), iota((128, 128), 1)
    home = ((row % 16) // 4) * 32 + (row // 16) * 4 + row % 4
    return flag(home == col)


def pack(chunk, q):
    tall = jnp.concatenate([chunk[:, 128 * c : 128 * c + 128] for c in range(4)], axis=0)
    return jnp.dot(q, tall, preferred_element_type=F32).astype(BF).reshape(8, 16, 128)


def unpack(packed, q):
    tall = lax.dot_general(q, packed.reshape(128, 128), TN, preferred_element_type=F32).astype(BF)
    return jnp.concatenate([tall[32 * c : 32 * c + 32] for c in range(4)], axis=1)


def kernel(
    tokens, ids, weight, place, gu, down,
    out, totals, got_gu, got_down,
    x_send, x_all, y_send, y_back, ext, w, wd, acc, acc_in, hid, mix,
    s_send, s_recv, x_sems, x_recv, h_send, h_recv, l_sem,
):
    dp, me = lax.axis_index("dp"), lax.axis_index("expert")
    yh, xx = dp // 4, lax.rem(dp, 4)
    ypeer = lax.rem(dp + 4, 8)
    spouse = lax.rem(me + 32, NE)

    barrier = pltpu.get_barrier_semaphore()

    def greet(i, carry):
        pl.semaphore_signal(barrier, inc=1, device_id={"expert": lax.rem(me + i, NE)}, device_id_type=MESH)
        return carry

    lax.fori_loop(1, NE, greet, 0)

    def greet_dp(i, carry):
        pl.semaphore_signal(barrier, inc=1, device_id={"dp": lax.rem(dp + i, 8)}, device_id_type=MESH)
        return carry

    lax.fori_loop(1, 8, greet_dp, 0)

    half = pl.multiple_of(yh * 2048, 2048)
    other = pl.multiple_of((1 - yh) * 2048, 2048)
    local = []
    for g in range(2):
        local.append(pltpu.make_async_copy(gu.at[0, g, :, pl.ds(half, 2048)], w.at[pl.ds(g * UNITS, UNITS)], l_sem.at[g]))
    local.append(pltpu.make_async_copy(down.at[0], wd, l_sem.at[2]))
    for c in local:
        c.start()

    onehot = jnp.zeros((TOK, NE), F32)
    wide_w = jnp.zeros((TOK, NE), F32)
    for k in range(8):
        hit = ids[:, k : k + 1] == iota((TOK, NE), 1)
        onehot = onehot + jnp.where(hit, 1.0, 0.0)
        wide_w = wide_w + jnp.where(hit, weight[:, k : k + 1], 0.0)
    perm = flag(place[...] == iota((NE, 128), 1))
    has = jnp.dot(onehot.astype(BF), perm, preferred_element_type=F32)
    before = flag(iota((TOK, TOK), 1) < iota((TOK, TOK), 0))
    count = jnp.dot(before, has.astype(BF), preferred_element_type=F32)
    pos = jnp.where(has > 0.5, count, -1.0).astype(BF)
    spread_m = flag(iota((128, NE * MAIN), 1) // MAIN == iota((128, NE * MAIN), 0))
    spread_x = flag(iota((128, NE * EXT), 1) // EXT == iota((128, NE * EXT), 0))
    row_m = (iota((TOK, NE * MAIN), 1) % MAIN).astype(F32)
    row_x = (iota((TOK, NE * EXT), 1) % EXT + MAIN).astype(F32)
    at_m = jnp.dot(pos, spread_m, preferred_element_type=F32) == row_m
    at_x = jnp.dot(pos, spread_x, preferred_element_type=F32) == row_x
    q = shuffle_matrix()
    x_send[:, :, :FEAT] = (
        lax.dot_general(flag(at_m), tokens[...], TN, preferred_element_type=F32).astype(BF).reshape(NE, MAIN, FEAT)
    )
    further = lax.dot_general(flag(at_x), tokens[...], TN, preferred_element_type=F32)
    tally = jnp.dot(flag(iota((NE * EXT, TOK), 0) % EXT == 3), has.astype(BF), preferred_element_type=F32)
    ext[:, :128] = (further[:, :128] + tally).astype(BF)
    ext[:, 128:] = further[:, 128:].astype(BF)
    for b in range(8):
        x_send[8 * b : 8 * b + 8, :, FEAT:] = pack(ext[32 * b : 32 * b + 32, :], q)

    pl.semaphore_wait(barrier, NE - 1 + 7)

    def send_rows(n, carry):
        step = (n + 1) // 2
        d = lax.rem(jnp.where(lax.rem(n, 2) == 1, me + step, me + NE - step), NE)
        pltpu.make_async_remote_copy(
            x_send.at[d], x_all.at[xx, me], s_send.at[0], s_recv.at[0], device_id={"expert": d}, device_id_type=MESH
        ).start()
        return carry

    lax.fori_loop(1, NE, send_rows, 0)
    mine = pltpu.make_async_copy(x_send.at[me], x_all.at[xx, me], l_sem.at[3])
    mine.start()
    trade = []
    for g in range(2):
        trade.append(
            pltpu.make_async_remote_copy(
                gu.at[0, g, :, pl.ds(other, 2048)], w.at[pl.ds((2 + g) * UNITS, UNITS)],
                s_send.at[1 + g], s_recv.at[1 + g], device_id={"dp": ypeer}, device_id_type=MESH,
            )
        )
    for c in trade:
        c.start()
    swap = [
        pltpu.make_async_remote_copy(gu, got_gu, s_send.at[3], s_recv.at[3], device_id={"expert": spouse}, device_id_type=MESH),
        pltpu.make_async_remote_copy(down, got_down, s_send.at[4], s_recv.at[4], device_id={"expert": spouse}, device_id_type=MESH),
    ]
    for c in swap:
        c.start()

    rest = wide_w
    for n in range(3):
        term = rest.astype(BF)
        rest = rest - term.astype(F32)
        by_slot = jnp.dot(term, perm, preferred_element_type=F32).astype(BF)
        mix[n, :, : NE * MAIN] = jnp.where(at_m, jnp.dot(by_slot, spread_m, preferred_element_type=F32), 0.0).astype(BF)
        mix[n, :, NE * MAIN :] = jnp.where(at_x, jnp.dot(by_slot, spread_x, preferred_element_type=F32), 0.0).astype(BF)
    acc[...] = jnp.zeros_like(acc)
    for c in local:
        c.wait()

    mine.wait()
    pltpu.make_async_copy(x_all.at[xx, pl.ds(0, NE - 1)], x_all.at[xx, pl.ds(0, NE - 1)], s_recv.at[0]).wait()

    def along_x(i):
        p = yh * 4 + lax.rem(xx + i, 4)
        return pltpu.make_async_remote_copy(
            x_all.at[xx], x_all.at[xx], x_sems.at[i - 1], x_recv.at[i - 1], device_id={"dp": p}, device_id_type=MESH
        )

    around = [along_x(1), along_x(3), along_x(2)]
    for c in around:
        c.start()
    for c in trade:
        c.wait_recv()

    def project(source):
        for b in range(8):
            ext[32 * b : 32 * b + 32, :] = unpack(x_all[source, 8 * b : 8 * b + 8, :, FEAT:], q)
        ww = w[:, pl.ds(pl.multiple_of(source * FEAT, FEAT), FEAT)]

        def tile(t, carry):
            rows = x_all[source, pl.ds(t * 16, 16), :, :FEAT].reshape(TILE, FEAT)
            acc[:, pl.ds(pl.multiple_of(t * TILE, TILE), TILE)] += lax.dot_general(ww, rows, NT, preferred_element_type=F32)
            return carry

        lax.fori_loop(0, 4, tile, 0)
        acc[:, 4 * TILE :] += lax.dot_general(ww, ext[...], NT, preferred_element_type=F32)

    project(xx)
    sel = flag(iota((8, NE * EXT), 1) % EXT == 3)
    totals[...] = jnp.dot(sel, ext[:, :128], preferred_element_type=F32)
    for i, c in ((1, around[0]), (3, around[1]), (2, around[2])):
        c.wait_recv()
        project(lax.rem(xx + 4 - i, 4))

    part = pltpu.make_async_remote_copy(
        acc.at[pl.ds(2 * UNITS, 2 * UNITS)], acc_in, s_send.at[5], s_recv.at[5], device_id={"dp": ypeer}, device_id_type=MESH
    )
    part.start()
    part.wait_recv()
    gate = acc[:UNITS, :] + acc_in[:UNITS, :]
    up = acc[UNITS : 2 * UNITS, :] + acc_in[UNITS:, :]
    here = pl.ds(pl.multiple_of(dp * UNITS, UNITS), UNITS)
    hid[here, :] = (gate / (1.0 + jnp.exp(-gate)) * up).astype(BF)

    def send_hidden(i, carry):
        pltpu.make_async_remote_copy(
            hid.at[here], hid.at[here], h_send, h_recv, device_id={"dp": lax.rem(dp + i, 8)}, device_id_type=MESH
        ).start()
        return carry

    lax.fori_loop(1, 8, send_hidden, 0)
    seven = hid.at[pl.ds(0, 7 * UNITS)]
    pltpu.make_async_copy(seven, seven, h_recv).wait()

    def produce(t):
        part = hid[:, pl.ds(pl.multiple_of(t * TILE, TILE), TILE)]
        return lax.dot_general(part, wd[...], TN, preferred_element_type=F32).astype(BF)

    def result(t, carry):
        y_send[pl.ds(t * 16, 16), :, :FEAT] = produce(t).reshape(16, MAIN, FEAT)
        return carry

    lax.fori_loop(0, 4, result, 0)
    ext[...] = produce(4)
    for b in range(8):
        y_send[8 * b : 8 * b + 8, :, FEAT:] = pack(ext[32 * b : 32 * b + 32, :], q)

    def send_back(n, carry):
        step = (n + 1) // 2
        d = lax.rem(jnp.where(lax.rem(n, 2) == 1, me + step, me + NE - step), NE)
        pltpu.make_async_remote_copy(
            y_send.at[d], y_back.at[me], s_send.at[6], s_recv.at[6], device_id={"expert": d}, device_id_type=MESH
        ).start()
        return carry

    lax.fori_loop(1, NE, send_back, 0)
    own = pltpu.make_async_copy(y_send.at[me], y_back.at[me], l_sem.at[3])
    own.start()
    own.wait()
    many = y_back.at[pl.ds(0, NE - 1)]
    pltpu.make_async_copy(many, many, s_recv.at[6]).wait()

    for b in range(8):
        ext[32 * b : 32 * b + 32, :] = unpack(y_back[8 * b : 8 * b + 8, :, FEAT:], q)
    rows = y_back[:, :, :FEAT].reshape(NE * MAIN, FEAT)
    total = jnp.zeros((TOK, FEAT), F32)
    for n in range(3):
        total = total + jnp.dot(mix[n, :, : NE * MAIN], rows, preferred_element_type=F32)
        total = total + jnp.dot(mix[n, :, NE * MAIN :], ext[...], preferred_element_type=F32)
    out[...] = total.astype(BF)

    sent = x_send.at[pl.ds(0, NE - 1)]
    pltpu.make_async_copy(sent, sent, s_send.at[0]).wait()
    pltpu.make_async_copy(sent, sent, s_send.at[6]).wait()
    pltpu.make_async_copy(seven, seven, h_send).wait()
    part.wait_send()
    for c in trade + around:
        c.wait_send()
    for c in swap:
        c.wait()


def body(tokens, expert_ids, route_weight, placement, swap_flag, gate_up, down_weight):
    vmem = pl.BlockSpec(memory_space=pltpu.VMEM)
    hbm = pl.BlockSpec(memory_space=pl.ANY)
    moe_out, totals, got_gu, got_down = pl.pallas_call(
        kernel,
        out_shape=[
            jax.ShapeDtypeStruct((TOK, FEAT), BF),
            jax.ShapeDtypeStruct((8, 128), F32),
            jax.ShapeDtypeStruct(gate_up.shape, BF),
            jax.ShapeDtypeStruct(down_weight.shape, BF),
        ],
        in_specs=[vmem, vmem, vmem, vmem, hbm, hbm],
        out_specs=[vmem, vmem, hbm, hbm],
        scratch_shapes=[
            pltpu.VMEM((NE, MAIN, WIDE), BF),
            pltpu.VMEM((4, NE, MAIN, WIDE), BF),
            pltpu.VMEM((NE, MAIN, WIDE), BF),
            pltpu.VMEM((NE, MAIN, WIDE), BF),
            pltpu.VMEM((NE * EXT, FEAT), BF),
            pltpu.VMEM((4 * UNITS, 4 * FEAT), BF),
            pltpu.VMEM((8 * UNITS, FEAT), BF),
            pltpu.VMEM((4 * UNITS, ROWS), F32),
            pltpu.VMEM((2 * UNITS, ROWS), F32),
            pltpu.VMEM((8 * UNITS, ROWS), BF),
            pltpu.VMEM((3, TOK, ROWS), BF),
            pltpu.SemaphoreType.DMA((7,)),
            pltpu.SemaphoreType.DMA((7,)),
            pltpu.SemaphoreType.DMA((3,)),
            pltpu.SemaphoreType.DMA((3,)),
            pltpu.SemaphoreType.DMA,
            pltpu.SemaphoreType.DMA,
            pltpu.SemaphoreType.DMA((4,)),
        ],
        compiler_params=pltpu.CompilerParams(
            collective_id=0, has_side_effects=True, vmem_limit_bytes=48 << 20
        ),
        cost_estimate=pl.CostEstimate(flops=5_000_000_000, bytes_accessed=10_000_000, transcendentals=200_000),
        name="experts",
    )(tokens, expert_ids, route_weight, placement.reshape(NE, 1), gate_up, down_weight)
    flags = jnp.concatenate([swap_flag, swap_flag]) == 1
    load = totals[0, :NE]
    column_load = jnp.where(flags, jnp.roll(load, NE // 2), load) / jnp.float32(TOK * 8)
    mine = jnp.arange(NE // 2, dtype=jnp.int32) == lax.axis_index("expert") % (NE // 2)
    swapped = jnp.sum(jnp.where(mine, swap_flag, 0)) == 1
    return (
        moe_out,
        column_load,
        jnp.where(swapped, got_gu, gate_up),
        jnp.where(swapped, got_down, down_weight),
    )


def solution(mesh):
    return jax.shard_map(
        body,
        mesh=mesh,
        in_specs=(
            P("expert", "dp"),
            P("expert", None),
            P("expert", None),
            P(),
            P(),
            P("expert", None, "dp", None),
            P("expert", None, "dp"),
        ),
        out_specs=(P("expert", "dp"), P(), P("expert", None, "dp", None), P("expert", None, "dp")),
        check_vma=False,
    )
```

time: 1090 us -> 369 us (0.34)
  waiting for transfers between devices: 779 us -> 0 us
  Pallas kernels: 0 us -> 354 us
  blocking collectives: 166 us -> 0 us
  local copies, waits for them, and re-layouts: 48.3 us -> 6.49 us
  starting transfers between devices: 41.3 us -> 0 us
  other arithmetic: 25.6 us -> 4.15 us
  between operations: 14.9 us -> 1.32 us
    ppermute x2 -> x0, waiting for transfers between devices: 699 us -> none  [from_behind(): return lax.ppermute(value, axis, pairs)]
    pallas_call x0 -> x1, Pallas kernels: none -> 354 us  [body(): pl.pallas_call(kernel, out_shape=[jax.ShapeDtypeStruct((TOK, FEAT), BF),...]
    psum x1 -> x0, blocking collectives: 166 us -> none  [body(): totals = lax.psum(local_counts, 'expert')]
    all_gather x2 -> x0, waiting for transfers between devices: 78.6 us -> none  [the longest x1 49.2 us: body(): whole = lax.all_gather(tokens, 'dp', axis=1, tiled=True)]
    all_to_all x2 -> x0, starting transfers between devices: 27.1 us -> none  [the longest x1 13.8 us: body(): lax.all_to_all(buffer, 'expert', split_axis=0, concat_axis=0, tiled=True)]
    reshape x4 -> x1, local copies, waits for them, and re-layouts: 25.6 us -> 0.75 us  [body(): placement.reshape(NE, 1)]
    another operation x2 -> x0, other arithmetic: 18 us -> none
    scatter x1 -> x0, local copies, waits for them, and re-layouts: 17.4 us -> none  [body(): jnp.zeros((ncol * capacity, width), jnp.bfloat16).at[slot_index]]
  transfers between devices with their start and end apart: 6 -> 0, of which waited for: 4 -> 0; matrix products, arithmetic and copies ran while one was open for 2% -> 0% of each run, Pallas kernels for 0% -> 0%
where the time goes in v1:
time: 369 us; the launch traced here: 366 us
  Pallas kernels  354 us (96%)
  local copies, waits for them, and re-layouts  6.49 us (2%)
  other arithmetic  4.15 us (1%)
    pallas_call x1, Pallas kernels, body(): pl.pallas_call(kernel, out_shape=[jax.ShapeDtypeStruct((TOK, FEAT), BF),...  354 us

profile of v1, /device:TPU:6, one launch (start us, length us, event | category | flops | bytes accessed | tf_op | source)
XLA Modules:
  0.0 366.2 jit_solution(16093260840268961137)
XLA Ops:
  0.6 1.3 fusion.1
  2.6 0.7 copy.13.place
  3.3 0.8 copy.11.ids
  4.1 0.8 copy.12.weight
  4.9 0.0 copy-start
  4.9 1.4 copy-done
  6.3 0.0 copy-start.1
  6.3 1.1 copy-done.1
  7.5 0.0 copy-start.2
  7.5 0.9 copy-done.2
  8.4 0.0 copy-start.3
  8.4 354.2 %experts.1 = (bf16[128,512]{1,0:T(8,128)(2,1)S(1)}, f32[8,128]{1,0:T(8,128)S(1)}, bf16[1,2,96,4096]{3,2,1,0:T(8,128)(2,1)S(1)}, bf16[1,768,512]{2,1,0:T(8,128)(2,1)S(1)}) custom-call(bf16[128,512]{1,0:T(8,128)(2,1)S(1)} %copy-done.2, s32[128,8]{1,0:T(8,128)S(1)} %copy.11.ids, f32[128,8]{1,0:T(8,128)S(1)} %copy.12.weight, s32[64,1]{1,0:T(8,128)S(1)} %copy.13.place, ...), custom_call_target="tpu_custom_call" | custom-call | flops 5000000000 | bytes 10000000 | tf_op jit(solution)/shard_map/experts/pallas_call | solution.py:257
  362.6 0.1 slice_bitcast_fusion.1
  362.7 0.0 copy-done.3
  362.7 0.6 fusion
  363.3 1.0 broadcast_select_fusion.1
  364.2 1.3 broadcast_select_fusion
  365.5 0.7 copy.15
Async XLA Ops:
  4.9 1.4 copy-start
  6.3 1.1 copy-start.1
  7.5 0.9 copy-start.2
  8.4 354.3 %copy-start.3 = (s32[32]{0:T(128)S(1)}, s32[32]{0:T(128)}, u32[]{:S(2)}) copy-start(s32[32]{0:T(128)} %param.11) | copy-start | bytes 388

commit v2 on v0

v2 whole, which is shorter than its diff:
```python
import jax
import jax.numpy as jnp
from jax import lax
from jax.experimental import pallas as pl
from jax.experimental.pallas import tpu as pltpu
from jax.sharding import PartitionSpec as P

MESH = pl.DeviceIdType.MESH
BF = jnp.bfloat16
F32 = jnp.float32
NN = (((1,), (0,)), ((), ()))
NT = (((1,), (1,)), ((), ()))
TN = (((0,), (0,)), ((), ()))

NE = 64
NZ = 16
TOK = 128
FEAT = 512
MAIN, EXT = 16, 4
WIDE = FEAT + 128
UNITS = 96
TILE = 256
TILES = 5


def iota(shape, axis):
    return lax.broadcasted_iota(jnp.int32, shape, axis)


def flag(cond):
    return jnp.where(cond, 1.0, 0.0).astype(BF)


def dot(a, b, dims=NN):
    return lax.dot_general(a, b, dims, preferred_element_type=F32)


def shuffle8():
    row, col = iota((128, 128), 0), iota((128, 128), 1)
    return flag(((row % 16) // 4) * 32 + (row // 16) * 4 + row % 4 == col)


def shuffle4():
    row, col = iota((64, 64), 0), iota((64, 64), 1)
    return flag(((row % 16) // 4) * 16 + (row // 16) * 4 + row % 4 == col)


def tall(rows):
    return jnp.concatenate([rows[:, 128 * c : 128 * c + 128] for c in range(4)], axis=0)


def broad(rows):
    n = rows.shape[0] // 4
    return jnp.concatenate([rows[n * c : n * c + n] for c in range(4)], axis=1)


def over_rows(values):
    row = iota((16, TOK), 0) // EXT
    last = sum(jnp.where(row == j, values[j], 0.0) for j in range(4))
    return jnp.concatenate([jnp.broadcast_to(v, (MAIN, TOK)) for v in values] + [last], axis=0)


def row_number():
    row = iota((80, TOK), 0)
    return jnp.where(row < 64, row % MAIN, MAIN + row % EXT).astype(F32)


def kernel(
    tokens, ids, weight, place, gu, down,
    out, totals, got_gu, got_down,
    ring, pick, x_all, wf, wd, p_send, p_own, p_in, hid, ext, y_send, y_in, up_out, up_in, dn_out, dn_in,
    snd, rcv, ru, rd, pr, hr, su, sd, loc,
):
    dp, me = lax.axis_index("dp"), lax.axis_index("expert")
    z, col = me // 4, lax.rem(me, 4)
    above, below = {"expert": lax.rem(me + 4, NE)}, {"expert": lax.rem(me + NE - 4, NE)}
    spouse = {"expert": lax.rem(me + 32, NE)}

    def near(i):
        return {"expert": z * 4 + lax.rem(col + i, 4)}

    def peer(i):
        return {"dp": lax.rem(dp + i, 8)}

    def remote(src, dst, send, recv, device):
        return pltpu.make_async_remote_copy(src, dst, send, recv, device_id=device, device_id_type=MESH)

    def await_bytes(ref, sem):
        pltpu.make_async_copy(ref, ref, sem).wait()

    barrier = pltpu.get_barrier_semaphore()
    others = [above, below, spouse] + [near(i) for i in (1, 2, 3)] + [peer(i) for i in range(1, 8)]
    for device in others:
        pl.semaphore_signal(barrier, inc=1, device_id=device, device_id_type=MESH)

    own_units = pl.ds(dp * 2, 2)
    own_feats = pl.ds(pl.multiple_of(dp * FEAT, FEAT), FEAT)
    local = [
        pltpu.make_async_copy(gu.at[0, :, :, own_feats], wf.at[own_units], loc.at[0]),
        pltpu.make_async_copy(down.at[0], wd, loc.at[1]),
    ]
    for c in local:
        c.start()

    lane = iota((TOK, 128), 1)
    place_f = place[...].astype(F32)
    hi = weight[...].astype(BF).astype(F32)
    lo = (weight[...] - hi).astype(BF).astype(F32)
    slots = []
    has = jnp.zeros((TOK, 128), F32)
    facts = jnp.zeros((TOK, 128), F32)
    for k in range(8):
        hit = ids[:, k : k + 1] == iota((TOK, NE), 1)
        slot = jnp.sum(jnp.where(hit, place_f, 0.0), axis=1, keepdims=True)
        slots.append(slot)
        has = has + jnp.where(slot == lane.astype(F32), 1.0, 0.0)
        facts = facts + jnp.where(lane == k, slot, 0.0)
        facts = facts + jnp.where(lane == 16 + k, hi[:, k : k + 1], 0.0) + jnp.where(lane == 24 + k, lo[:, k : k + 1], 0.0)
    before = flag(iota((TOK, TOK), 1) < iota((TOK, TOK), 0))
    count = dot(before, has.astype(BF))
    for k in range(8):
        pos = jnp.sum(jnp.where(slots[k] == lane.astype(F32), count, 0.0), axis=1, keepdims=True)
        facts = facts + jnp.where(lane == 8 + k, pos, 0.0)
    turned = dot(facts.astype(BF), flag(iota((TOK, TOK), 0) == iota((TOK, TOK), 1)), TN).astype(BF)
    ring[z, :TOK, :] = tokens[...]
    ring[z, TOK:, 0:128] = turned[0:16]
    ring[z, TOK:, 128:256] = turned[16:32]
    ring[z, TOK:, 256:384] = jnp.zeros((16, 128), BF)
    ring[z, TOK:, 384:512] = dot(flag(iota((16, TOK), 0) == 0), has.astype(BF)).astype(BF)

    pl.semaphore_wait(barrier, len(others))

    def pass_up(block, s):
        remote(ring.at[block], ring.at[block], snd.at[0], ru.at[s], above).start()

    def pass_down(block, s):
        remote(ring.at[block], ring.at[block], snd.at[1], rd.at[s], below).start()

    pass_up(z, 0)
    pass_down(z, 0)

    def send_weights(i, carry):
        p = lax.rem(dp + i, 8)
        feats = pl.ds(pl.multiple_of(p * FEAT, FEAT), FEAT)
        remote(gu.at[0, :, :, feats], wf.at[own_units], snd.at[3], rcv.at[1], {"dp": p}).start()
        return carry

    lax.fori_loop(1, 8, send_weights, 0)
    swap = [
        remote(gu, got_gu, snd.at[9], rcv.at[3], spouse),
        remote(down, got_down, snd.at[10], rcv.at[4], spouse),
    ]
    for c in swap:
        c.start()

    def by_slot(facts, values):
        return [
            jnp.sum(jnp.where(facts == (z * 4 + j).astype(F32), values, 0.0), axis=0, keepdims=True) for j in range(4)
        ]

    def picked(block):
        facts = ring[block, TOK:, 0:128].astype(F32)
        slot = facts[0:8]
        places = [v - 1.0 for v in by_slot(slot, facts[8:16] + 1.0)]
        return slot, over_rows(places) == row_number()

    def choose(block):
        rows = dot(flag(picked(block)[1]), ring[block, :TOK, :])
        more = rows[64:]
        third = flag((iota((16, 16), 0) % EXT == 3) & (iota((16, 16), 1) == 0))
        tally = dot(third, ring[block, TOK:, 384:512])
        more = tall(jnp.concatenate([more[:, :128] + tally, more[:, 128:]], axis=1)).astype(BF)
        pick[:, block, :, :FEAT] = rows[:64].astype(BF).reshape(4, MAIN, FEAT)
        pick[:, block, :, FEAT:] = dot(shuffle4(), more).astype(BF).reshape(4, MAIN, 128)
        to = col * NZ + block
        for i in (1, 2, 3):
            j = lax.rem(col + i, 4)
            remote(pick.at[j, block], x_all.at[to], snd.at[2], rcv.at[0], near(i)).start()
        pltpu.make_async_copy(pick.at[col, block], x_all.at[to], loc.at[2]).start()

    choose(z)

    def around(s, carry):
        low, high = lax.rem(z + 15 - s, NZ), lax.rem(z + 1 + s, NZ)
        await_bytes(ring.at[low], ru.at[s])
        pass_up(low, s + 1)
        await_bytes(ring.at[high], rd.at[s])

        @pl.when(s < 6)
        def _():
            pass_down(high, s + 1)

        choose(low)
        choose(high)
        return carry

    lax.fori_loop(0, 7, around, 0)
    far = lax.rem(z + 8, NZ)
    await_bytes(ring.at[far], ru.at[7])
    choose(far)

    for c in local:
        c.wait()
    await_bytes(wf.at[pl.ds(0, 14)], rcv.at[1])
    await_bytes(x_all.at[pl.ds(0, 48)], rcv.at[0])
    await_bytes(x_all.at[pl.ds(0, 16)], loc.at[2])

    q8 = shuffle8()
    for b in range(8):
        packed = x_all[8 * b : 8 * b + 8, :, FEAT:].reshape(128, 128)
        ext[32 * b : 32 * b + 32, :] = broad(dot(q8, packed, TN).astype(BF))
    totals[...] = dot(flag(iota((8, NE * EXT), 1) % EXT == 3), ext[:, :128])

    def project(t, rows):
        def one(i, carry):
            p = lax.rem(dp + i, 8)
            p_send[p, t] = dot(wf[pl.ds(p * 2, 2)].reshape(2 * UNITS, FEAT), rows, NT).astype(BF)
            remote(p_send.at[p, t], p_in.at[dp, t], snd.at[4], pr.at[t], {"dp": p}).start()
            return carry

        lax.fori_loop(1, 8, one, 0)
        p_own[t] = dot(wf[own_units].reshape(2 * UNITS, FEAT), rows, NT)

    def project_tile(t, carry):
        project(t, x_all[pl.ds(t * 16, 16), :, :FEAT].reshape(TILE, FEAT))
        return carry

    project(4, ext[...])
    lax.fori_loop(0, 4, project_tile, 0)

    def activate(n, carry):
        t = lax.rem(n + 4, TILES)
        await_bytes(p_in.at[pl.ds(0, 7), t], pr.at[t])
        both = p_own[t]
        for i in range(1, 8):
            both = both + p_in[lax.rem(dp + i, 8), t].astype(F32)
        gate, up = both[:UNITS], both[UNITS:]
        hid[t, dp] = (gate / (1.0 + jnp.exp(-gate)) * up).astype(BF)
        for i in range(1, 8):
            remote(hid.at[t, dp], hid.at[t, dp], snd.at[5], hr.at[t], peer(i)).start()
        return carry

    lax.fori_loop(0, TILES, activate, 0)

    def produce(t):
        await_bytes(hid.at[t, pl.ds(0, 7)], hr.at[t])
        return dot(hid[t].reshape(8 * UNITS, TILE), wd[...], TN).astype(BF)

    ext[...] = produce(4)

    def finish(j):
        rows = pl.ds(j * 16, 16)
        y_send[rows, :, :FEAT] = produce(j).reshape(16, MAIN, FEAT)
        for g in range(2):
            more = tall(ext[pl.ds(pl.multiple_of(j * 64 + g * 32, 32), 32), :])
            y_send[pl.ds(j * 16 + g * 8, 8), :, FEAT:] = dot(q8, more).astype(BF).reshape(8, MAIN, 128)
        return y_send.at[rows]

    def give_back(i, carry):
        ref = finish(lax.rem(col + i, 4))
        remote(ref, y_in.at[col], snd.at[6], rcv.at[2], near(i)).start()
        return carry

    lax.fori_loop(1, 4, give_back, 0)
    mine = pltpu.make_async_copy(finish(col), y_in.at[col], loc.at[3])
    mine.start()
    await_bytes(y_in.at[pl.ds(0, 3)], rcv.at[2])
    mine.wait()

    def combine(block):
        slot, at = picked(block)
        terms = ring[block, TOK:, 128:256].astype(F32)
        more = broad(dot(shuffle4(), y_in[:, block, :, FEAT:].reshape(64, 128), TN).astype(BF))
        rows = jnp.concatenate([y_in[:, block, :, :FEAT].reshape(64, FEAT), more], axis=0)
        share = jnp.zeros((TOK, FEAT), F32)
        for n in range(2):
            mix = jnp.where(at, over_rows(by_slot(slot, terms[8 * n : 8 * n + 8])), 0.0)
            share = share + dot(mix.astype(BF), rows, TN)
        return share

    def hand_up(s, total):
        up_out[s] = total.astype(BF)
        remote(up_out.at[s], up_in.at[s], snd.at[7], su.at[s], above).start()

    def hand_down(s, total):
        dn_out[s] = total.astype(BF)
        remote(dn_out.at[s], dn_in.at[s], snd.at[8], sd.at[s], below).start()

    hand_up(0, combine(far))
    hand_down(0, combine(lax.rem(z + 9, NZ)))

    def home(s, carry):
        share = combine(lax.rem(z + 8 - s, NZ))
        await_bytes(up_in.at[s - 1], su.at[s - 1])
        hand_up(s, share + up_in[s - 1].astype(F32))
        share = combine(lax.rem(z + 9 + s, NZ))
        await_bytes(dn_in.at[s - 1], sd.at[s - 1])
        hand_down(s, share + dn_in[s - 1].astype(F32))
        return carry

    lax.fori_loop(1, 7, home, 0)
    share = combine(lax.rem(z + 1, NZ))
    await_bytes(up_in.at[6], su.at[6])
    hand_up(7, share + up_in[6].astype(F32))
    share = combine(z)
    await_bytes(dn_in.at[6], sd.at[6])
    share = share + dn_in[6].astype(F32)
    await_bytes(up_in.at[7], su.at[7])
    out[...] = (share + up_in[7].astype(F32)).astype(BF)

    await_bytes(ring.at[pl.ds(0, 8)], snd.at[0])
    await_bytes(ring.at[pl.ds(0, 7)], snd.at[1])
    await_bytes(x_all.at[pl.ds(0, 48)], snd.at[2])
    await_bytes(wf.at[pl.ds(0, 14)], snd.at[3])
    await_bytes(p_in.at[pl.ds(0, 7)], snd.at[4])
    await_bytes(hid.at[:, pl.ds(0, 7)], snd.at[5])
    await_bytes(y_in.at[pl.ds(0, 3)], snd.at[6])
    await_bytes(up_out, snd.at[7])
    await_bytes(dn_out, snd.at[8])
    for c in swap:
        c.wait()


def body(tokens, expert_ids, route_weight, placement, swap_flag, gate_up, down_weight):
    vmem = pl.BlockSpec(memory_space=pltpu.VMEM)
    hbm = pl.BlockSpec(memory_space=pl.ANY)
    moe_out, totals, got_gu, got_down = pl.pallas_call(
        kernel,
        out_shape=[
            jax.ShapeDtypeStruct((TOK, FEAT), BF),
            jax.ShapeDtypeStruct((8, 128), F32),
            jax.ShapeDtypeStruct(gate_up.shape, BF),
            jax.ShapeDtypeStruct(down_weight.shape, BF),
        ],
        in_specs=[vmem, vmem, vmem, vmem, hbm, hbm],
        out_specs=[vmem, vmem, hbm, hbm],
        scratch_shapes=[
            pltpu.VMEM((NZ, TOK + 16, FEAT), BF),
            pltpu.VMEM((4, NZ, MAIN, WIDE), BF),
            pltpu.VMEM((NE, MAIN, WIDE), BF),
            pltpu.VMEM((16, UNITS, FEAT), BF),
            pltpu.VMEM((8 * UNITS, FEAT), BF),
            pltpu.VMEM((8, TILES, 2 * UNITS, TILE), BF),
            pltpu.VMEM((TILES, 2 * UNITS, TILE), F32),
            pltpu.VMEM((8, TILES, 2 * UNITS, TILE), BF),
            pltpu.VMEM((TILES, 8, UNITS, TILE), BF),
            pltpu.VMEM((NE * EXT, FEAT), BF),
            pltpu.VMEM((NE, MAIN, WIDE), BF),
            pltpu.VMEM((4, NZ, MAIN, WIDE), BF),
            pltpu.VMEM((8, TOK, FEAT), BF),
            pltpu.VMEM((8, TOK, FEAT), BF),
            pltpu.VMEM((7, TOK, FEAT), BF),
            pltpu.VMEM((7, TOK, FEAT), BF),
            pltpu.SemaphoreType.DMA((11,)),
            pltpu.SemaphoreType.DMA((5,)),
            pltpu.SemaphoreType.DMA((8,)),
            pltpu.SemaphoreType.DMA((7,)),
            pltpu.SemaphoreType.DMA((TILES,)),
            pltpu.SemaphoreType.DMA((TILES,)),
            pltpu.SemaphoreType.DMA((8,)),
            pltpu.SemaphoreType.DMA((7,)),
            pltpu.SemaphoreType.DMA((4,)),
        ],
        compiler_params=pltpu.CompilerParams(
            collective_id=0, has_side_effects=True, vmem_limit_bytes=48 << 20
        ),
        cost_estimate=pl.CostEstimate(flops=5_000_000_000, bytes_accessed=10_000_000, transcendentals=200_000),
        name="experts",
    )(tokens, expert_ids, route_weight, placement.reshape(1, NE), gate_up, down_weight)
    flags = jnp.concatenate([swap_flag, swap_flag]) == 1
    load = totals[0, :NE]
    column_load = jnp.where(flags, jnp.roll(load, NE // 2), load) / jnp.float32(TOK * 8)
    mine = jnp.arange(NE // 2, dtype=jnp.int32) == lax.axis_index("expert") % (NE // 2)
    swapped = jnp.sum(jnp.where(mine, swap_flag, 0)) == 1
    return (
        moe_out,
        column_load,
        jnp.where(swapped, got_gu, gate_up),
        jnp.where(swapped, got_down, down_weight),
    )


def solution(mesh):
    return jax.shard_map(
        body,
        mesh=mesh,
        in_specs=(
            P("expert", "dp"),
            P("expert", None),
            P("expert", None),
            P(),
            P(),
            P("expert", None, "dp", None),
            P("expert", None, "dp"),
        ),
        out_specs=(P("expert", "dp"), P(), P("expert", None, "dp", None), P("expert", None, "dp")),
        check_vma=False,
    )
```

time: 1090 us -> 388 us (0.36)
  waiting for transfers between devices: 779 us -> 0 us
  Pallas kernels: 0 us -> 374 us
  blocking collectives: 166 us -> 0 us
  local copies, waits for them, and re-layouts: 48.3 us -> 6.4 us
  starting transfers between devices: 41.3 us -> 0 us
  other arithmetic: 25.6 us -> 4.15 us
  between operations: 14.9 us -> 1.32 us
    ppermute x2 -> x0, waiting for transfers between devices: 699 us -> none  [from_behind(): return lax.ppermute(value, axis, pairs)]
    pallas_call x0 -> x1, Pallas kernels: none -> 374 us  [body(): pl.pallas_call(kernel, out_shape=[jax.ShapeDtypeStruct((TOK, FEAT), BF),...]
    psum x1 -> x0, blocking collectives: 166 us -> none  [body(): totals = lax.psum(local_counts, 'expert')]
    all_gather x2 -> x0, waiting for transfers between devices: 78.6 us -> none  [the longest x1 49.2 us: body(): whole = lax.all_gather(tokens, 'dp', axis=1, tiled=True)]
    all_to_all x2 -> x0, starting transfers between devices: 27.1 us -> none  [the longest x1 13.8 us: body(): lax.all_to_all(buffer, 'expert', split_axis=0, concat_axis=0, tiled=True)]
    reshape x4 -> x0, local copies, waits for them, and re-layouts: 25.6 us -> none  [the longest x1 12.3 us: body(): rows = received.reshape(blocks * count, wide)]
    another operation x2 -> x0, other arithmetic: 18 us -> none
    scatter x1 -> x0, local copies, waits for them, and re-layouts: 17.4 us -> none  [body(): jnp.zeros((ncol * capacity, width), jnp.bfloat16).at[slot_index]]
  transfers between devices with their start and end apart: 6 -> 0, of which waited for: 4 -> 0; matrix products, arithmetic and copies ran while one was open for 2% -> 0% of each run, Pallas kernels for 0% -> 0%
where the time goes in v2:
time: 388 us; the launch traced here: 386 us
  Pallas kernels  374 us (96%)
  local copies, waits for them, and re-layouts  6.4 us (2%)
  other arithmetic  4.15 us (1%)
    pallas_call x1, Pallas kernels, body(): pl.pallas_call(kernel, out_shape=[jax.ShapeDtypeStruct((TOK, FEAT), BF),...  374 us

profile of v2, /device:TPU:6, one launch (start us, length us, event | category | flops | bytes accessed | tf_op | source)
XLA Modules:
  0.0 385.6 jit_solution(10730303442903960444)
XLA Ops:
  0.6 1.3 fusion.1
  2.6 0.8 copy.11.ids
  3.4 0.8 copy.12.weight
  4.2 0.0 copy-start
  4.2 1.4 copy-done
  5.6 0.0 copy-start.1
  5.6 1.1 copy-done.1
  6.7 0.0 copy-start.2
  6.7 0.9 copy-done.2
  7.6 0.0 copy-start.3
  7.6 0.7 copy-done.3
  8.3 0.0 copy-start.4
  8.3 373.7 %experts.1 = (bf16[128,512]{1,0:T(8,128)(2,1)S(1)}, f32[8,128]{1,0:T(8,128)S(1)}, bf16[1,2,96,4096]{3,2,1,0:T(8,128)(2,1)S(1)}, bf16[1,768,512]{2,1,0:T(8,128)(2,1)S(1)}) custom-call(bf16[128,512]{1,0:T(8,128)(2,1)S(1)} %copy-done.2, s32[128,8]{1,0:T(8,128)S(1)} %copy.11.ids, f32[128,8]{1,0:T(8,128)S(1)} %copy.12.weight, s32[1,64]{1,0:T(1,128)S(1)} %bitcast.7, ...), custom_call_target="tpu_custom_call" | custom-call | flops 5000000000 | bytes 10000000 | tf_op jit(solution)/shard_map/experts/pallas_call | solution.py:327
  382.0 0.1 slice_bitcast_fusion.1
  382.1 0.0 copy-done.4
  382.1 0.6 fusion
  382.7 1.0 broadcast_select_fusion.1
  383.6 1.3 broadcast_select_fusion
  384.9 0.7 copy.14
Async XLA Ops:
  4.2 1.4 copy-start
  5.6 1.1 copy-start.1
  6.7 0.9 copy-start.2
  7.6 0.7 copy-start.3
  8.3 373.8 %copy-start.4 = (s32[32]{0:T(128)S(1)}, s32[32]{0:T(128)}, u32[]{:S(2)}) copy-start(s32[32]{0:T(128)} %param.11) | copy-start | bytes 388

commit v3 on v2

--- a/solution.py
+++ b/solution.py
@@ -1,3 +1,5 @@
+import functools
+
 import jax
 import jax.numpy as jnp
 from jax import lax
@@ -67,8 +69,8 @@
 
 def kernel(
     tokens, ids, weight, place, gu, down,
-    out, totals, got_gu, got_down,
-    ring, pick, x_all, wf, wd, p_send, p_own, p_in, hid, ext, y_send, y_in, up_out, up_in, dn_out, dn_in,
+    out, totals, got_gu,
+    ring, pick, x_all, w, wd, p_send, p_own, p_in, hid, ext, y_send, y_in, up_out, up_in, dn_out, dn_in,
     snd, rcv, ru, rd, pr, hr, su, sd, loc,
 ):
     dp, me = lax.axis_index("dp"), lax.axis_index("expert")
@@ -76,8 +78,11 @@
     above, below = {"expert": lax.rem(me + 4, NE)}, {"expert": lax.rem(me + NE - 4, NE)}
     spouse = {"expert": lax.rem(me + 32, NE)}
 
-    def near(i):
-        return {"expert": z * 4 + lax.rem(col + i, 4)}
+    yh, xx = dp // 4, lax.rem(dp, 4)
+    across = {"dp": lax.rem(dp + 4, 8)}
+
+    def near(i, k=0):
+        return {"dp": yh * 4 + lax.rem(xx + k, 4), "expert": z * 4 + lax.rem(col + i, 4)}
 
     def peer(i):
         return {"dp": lax.rem(dp + i, 8)}
@@ -89,14 +94,15 @@
         pltpu.make_async_copy(ref, ref, sem).wait()
 
     barrier = pltpu.get_barrier_semaphore()
-    others = [above, below, spouse] + [near(i) for i in (1, 2, 3)] + [peer(i) for i in range(1, 8)]
+    others = [above, below, spouse] + [near(n % 4, n // 4) for n in range(1, 16)]
+    others += [{"dp": (1 - yh) * 4 + lax.rem(xx + k, 4)} for k in range(4)]
     for device in others:
         pl.semaphore_signal(barrier, inc=1, device_id=device, device_id_type=MESH)
 
-    own_units = pl.ds(dp * 2, 2)
-    own_feats = pl.ds(pl.multiple_of(dp * FEAT, FEAT), FEAT)
+    half = pl.ds(pl.multiple_of(yh * 2048, 2048), 2048)
+    other_half = pl.ds(pl.multiple_of((1 - yh) * 2048, 2048), 2048)
     local = [
-        pltpu.make_async_copy(gu.at[0, :, :, own_feats], wf.at[own_units], loc.at[0]),
+        pltpu.make_async_copy(gu.at[0, :, :, half], w.at[pl.ds(0, 2)], loc.at[0]),
         pltpu.make_async_copy(down.at[0], wd, loc.at[1]),
     ]
     for c in local:
@@ -126,6 +132,7 @@
     ring[z, TOK:, 0:128] = turned[0:16]
     ring[z, TOK:, 128:256] = turned[16:32]
     ring[z, TOK:, 256:384] = jnp.zeros((16, 128), BF)
+    early = remote(gu.at[0, 0], got_gu.at[0, 0], snd.at[9], rcv.at[3], spouse)
     ring[z, TOK:, 384:512] = dot(flag(iota((16, TOK), 0) == 0), has.astype(BF)).astype(BF)
 
     pl.semaphore_wait(barrier, len(others))
@@ -139,19 +146,8 @@
     pass_up(z, 0)
     pass_down(z, 0)
 
-    def send_weights(i, carry):
-        p = lax.rem(dp + i, 8)
-        feats = pl.ds(pl.multiple_of(p * FEAT, FEAT), FEAT)
-        remote(gu.at[0, :, :, feats], wf.at[own_units], snd.at[3], rcv.at[1], {"dp": p}).start()
-        return carry
-
-    lax.fori_loop(1, 8, send_weights, 0)
-    swap = [
-        remote(gu, got_gu, snd.at[9], rcv.at[3], spouse),
-        remote(down, got_down, snd.at[10], rcv.at[4], spouse),
-    ]
-    for c in swap:
-        c.start()
+    trade = remote(gu.at[0, :, :, other_half], w.at[pl.ds(2, 2)], snd.at[3], rcv.at[1], across)
+    trade.start()
 
     def by_slot(facts, values):
         return [
@@ -164,21 +160,25 @@
         places = [v - 1.0 for v in by_slot(slot, facts[8:16] + 1.0)]
         return slot, over_rows(places) == row_number()
 
-    def choose(block):
+    def choose(block, n):
         rows = dot(flag(picked(block)[1]), ring[block, :TOK, :])
         more = rows[64:]
         third = flag((iota((16, 16), 0) % EXT == 3) & (iota((16, 16), 1) == 0))
         tally = dot(third, ring[block, TOK:, 384:512])
         more = tall(jnp.concatenate([more[:, :128] + tally, more[:, 128:]], axis=1)).astype(BF)
-        pick[:, block, :, :FEAT] = rows[:64].astype(BF).reshape(4, MAIN, FEAT)
-        pick[:, block, :, FEAT:] = dot(shuffle4(), more).astype(BF).reshape(4, MAIN, 128)
-        to = col * NZ + block
-        for i in (1, 2, 3):
+        pick[:, n, :, :FEAT] = rows[:64].astype(BF).reshape(4, MAIN, FEAT)
+        pick[:, n, :, FEAT:] = dot(shuffle4(), more).astype(BF).reshape(4, MAIN, 128)
+
+    def deal(n, blocks):
+        src, dst = pl.ds(n, blocks), pl.ds(xx * NE + col * NZ + n, blocks)
+        for m in range(1, 16):
+            i, k = m % 4, m // 4
             j = lax.rem(col + i, 4)
-            remote(pick.at[j, block], x_all.at[to], snd.at[2], rcv.at[0], near(i)).start()
-        pltpu.make_async_copy(pick.at[col, block], x_all.at[to], loc.at[2]).start()
-
-    choose(z)
+            remote(pick.at[j, src], x_all.at[dst], snd.at[2], rcv.at[0], near(i, k)).start()
+        pltpu.make_async_copy(pick.at[col, src], x_all.at[dst], loc.at[2]).start()
+
+    choose(z, 0)
+    deal(0, 1)
 
     def around(s, carry):
         low, high = lax.rem(z + 15 - s, NZ), lax.rem(z + 1 + s, NZ)
@@ -190,50 +190,54 @@
         def _():
             pass_down(high, s + 1)
 
-        choose(low)
-        choose(high)
+        choose(low, 2 * s + 1)
+        choose(high, 2 * s + 2)
+        deal(2 * s + 1, 2)
         return carry
 
     lax.fori_loop(0, 7, around, 0)
     far = lax.rem(z + 8, NZ)
     await_bytes(ring.at[far], ru.at[7])
-    choose(far)
+    choose(far, 15)
+    deal(15, 1)
 
     for c in local:
         c.wait()
-    await_bytes(wf.at[pl.ds(0, 14)], rcv.at[1])
-    await_bytes(x_all.at[pl.ds(0, 48)], rcv.at[0])
-    await_bytes(x_all.at[pl.ds(0, 16)], loc.at[2])
+    trade.wait_recv()
+    await_bytes(x_all.at[pl.ds(0, 15 * NZ)], rcv.at[0])
+    await_bytes(x_all.at[pl.ds(0, NZ)], loc.at[2])
+    early.start()
 
     q8 = shuffle8()
-    for b in range(8):
-        packed = x_all[8 * b : 8 * b + 8, :, FEAT:].reshape(128, 128)
-        ext[32 * b : 32 * b + 32, :] = broad(dot(q8, packed, TN).astype(BF))
-    totals[...] = dot(flag(iota((8, NE * EXT), 1) % EXT == 3), ext[:, :128])
-
-    def project(t, rows):
-        def one(i, carry):
-            p = lax.rem(dp + i, 8)
-            p_send[p, t] = dot(wf[pl.ds(p * 2, 2)].reshape(2 * UNITS, FEAT), rows, NT).astype(BF)
-            remote(p_send.at[p, t], p_in.at[dp, t], snd.at[4], pr.at[t], {"dp": p}).start()
-            return carry
-
-        lax.fori_loop(1, 8, one, 0)
-        p_own[t] = dot(wf[own_units].reshape(2 * UNITS, FEAT), rows, NT)
+
+    def project(t, rows_of):
+        total = jnp.zeros((4 * UNITS, TILE), F32)
+        for x in range(4):
+            part = w[:, :, x * FEAT : x * FEAT + FEAT].reshape(4 * UNITS, FEAT)
+            total = total + dot(part, rows_of(x), NT)
+        p_own[t] = total[: 2 * UNITS]
+        p_send[t] = total[2 * UNITS :]
+        remote(p_send.at[t], p_in.at[t], snd.at[4], pr.at[t], across).start()
+
+    def further_rows(x):
+        for b in range(8):
+            packed = x_all[x * NE + 8 * b : x * NE + 8 * b + 8, :, FEAT:].reshape(128, 128)
+            ext[32 * b : 32 * b + 32, :] = broad(dot(q8, packed, TN).astype(BF))
+        if x == 0:
+            totals[...] = dot(flag(iota((8, NE * EXT), 1) % EXT == 3), ext[:, :128])
+        return ext[...]
 
     def project_tile(t, carry):
-        project(t, x_all[pl.ds(t * 16, 16), :, :FEAT].reshape(TILE, FEAT))
+        project(t, lambda x: x_all[pl.ds(x * NE + t * 16, 16), :, :FEAT].reshape(TILE, FEAT))
         return carry
 
-    project(4, ext[...])
+    project(4, further_rows)
     lax.fori_loop(0, 4, project_tile, 0)
 
     def activate(n, carry):
         t = lax.rem(n + 4, TILES)
-        await_bytes(p_in.at[pl.ds(0, 7), t], pr.at[t])
-        both = p_own[t]
-        for i in range(1, 8):
-            both = both + p_in[lax.rem(dp + i, 8), t].astype(F32)
+        await_bytes(p_in.at[t], pr.at[t])
+        both = p_own[t] + p_in[t]
         gate, up = both[:UNITS], both[UNITS:]
         hid[t, dp] = (gate / (1.0 + jnp.exp(-gate)) * up).astype(BF)
         for i in range(1, 8):
@@ -267,14 +271,14 @@
     await_bytes(y_in.at[pl.ds(0, 3)], rcv.at[2])
     mine.wait()
 
-    def combine(block):
+    def combine(block, n):
         slot, at = picked(block)
         terms = ring[block, TOK:, 128:256].astype(F32)
-        more = broad(dot(shuffle4(), y_in[:, block, :, FEAT:].reshape(64, 128), TN).astype(BF))
-        rows = jnp.concatenate([y_in[:, block, :, :FEAT].reshape(64, FEAT), more], axis=0)
+        more = broad(dot(shuffle4(), y_in[:, n, :, FEAT:].reshape(64, 128), TN).astype(BF))
+        rows = jnp.concatenate([y_in[:, n, :, :FEAT].reshape(64, FEAT), more], axis=0)
         share = jnp.zeros((TOK, FEAT), F32)
-        for n in range(2):
-            mix = jnp.where(at, over_rows(by_slot(slot, terms[8 * n : 8 * n + 8])), 0.0)
+        for part in range(2):
+            mix = jnp.where(at, over_rows(by_slot(slot, terms[8 * part : 8 * part + 8])), 0.0)
             share = share + dot(mix.astype(BF), rows, TN)
         return share
 
@@ -286,23 +290,23 @@
         dn_out[s] = total.astype(BF)
         remote(dn_out.at[s], dn_in.at[s], snd.at[8], sd.at[s], below).start()
 
-    hand_up(0, combine(far))
-    hand_down(0, combine(lax.rem(z + 9, NZ)))
+    hand_up(0, combine(far, 15))
+    hand_down(0, combine(lax.rem(z + 9, NZ), 13))
 
     def home(s, carry):
-        share = combine(lax.rem(z + 8 - s, NZ))
+        share = combine(lax.rem(z + 8 - s, NZ), 16 - 2 * s)
         await_bytes(up_in.at[s - 1], su.at[s - 1])
         hand_up(s, share + up_in[s - 1].astype(F32))
-        share = combine(lax.rem(z + 9 + s, NZ))
+        share = combine(lax.rem(z + 9 + s, NZ), 13 - 2 * s)
         await_bytes(dn_in.at[s - 1], sd.at[s - 1])
         hand_down(s, share + dn_in[s - 1].astype(F32))
         return carry
 
     lax.fori_loop(1, 7, home, 0)
-    share = combine(lax.rem(z + 1, NZ))
+    share = combine(lax.rem(z + 1, NZ), 2)
     await_bytes(up_in.at[6], su.at[6])
     hand_up(7, share + up_in[6].astype(F32))
-    share = combine(z)
+    share = combine(z, 0)
     await_bytes(dn_in.at[6], sd.at[6])
     share = share + dn_in[6].astype(F32)
     await_bytes(up_in.at[7], su.at[7])
@@ -310,39 +314,72 @@
 
     await_bytes(ring.at[pl.ds(0, 8)], snd.at[0])
     await_bytes(ring.at[pl.ds(0, 7)], snd.at[1])
-    await_bytes(x_all.at[pl.ds(0, 48)], snd.at[2])
-    await_bytes(wf.at[pl.ds(0, 14)], snd.at[3])
-    await_bytes(p_in.at[pl.ds(0, 7)], snd.at[4])
+    await_bytes(x_all.at[pl.ds(0, 15 * NZ)], snd.at[2])
+    trade.wait_send()
+    await_bytes(p_in, snd.at[4])
     await_bytes(hid.at[:, pl.ds(0, 7)], snd.at[5])
     await_bytes(y_in.at[pl.ds(0, 3)], snd.at[6])
     await_bytes(up_out, snd.at[7])
     await_bytes(dn_out, snd.at[8])
-    for c in swap:
-        c.wait()
+    early.wait()
+
+
+def exchange_kernel(pair, gu, down, old_gu, old_down, got_gu, got_down, snd, rcv):
+    me = lax.axis_index("expert")
+    spouse = {"expert": lax.rem(me + NE // 2, NE)}
+
+    @pl.when(lax.rem(me, NE // 2) == pair)
+    def _():
+        barrier = pltpu.get_barrier_semaphore()
+        pl.semaphore_signal(barrier, inc=1, device_id=spouse, device_id_type=MESH)
+        pl.semaphore_wait(barrier, 1)
+        copies = [
+            pltpu.make_async_remote_copy(src, dst, snd.at[n], rcv.at[n], device_id=spouse, device_id_type=MESH)
+            for n, (src, dst) in enumerate([(gu.at[0, 1], got_gu.at[0, 1]), (down, got_down)])
+        ]
+        for c in copies:
+            c.start()
+        for c in copies:
+            c.wait()
+
+
+def exchange(pair, gu, down, old_gu, old_down):
+    hbm = pl.BlockSpec(memory_space=pl.ANY)
+    return tuple(
+        pl.pallas_call(
+            functools.partial(exchange_kernel, pair),
+            out_shape=[jax.ShapeDtypeStruct(old_gu.shape, BF), jax.ShapeDtypeStruct(old_down.shape, BF)],
+            in_specs=[hbm] * 4,
+            out_specs=[hbm] * 2,
+            input_output_aliases={2: 0, 3: 1},
+            scratch_shapes=[pltpu.SemaphoreType.DMA((2,)), pltpu.SemaphoreType.DMA((2,))],
+            compiler_params=pltpu.CompilerParams(collective_id=1 + pair, has_side_effects=True),
+            name="exchange",
+        )(gu, down, old_gu, old_down)
+    )
 
 
 def body(tokens, expert_ids, route_weight, placement, swap_flag, gate_up, down_weight):
     vmem = pl.BlockSpec(memory_space=pltpu.VMEM)
     hbm = pl.BlockSpec(memory_space=pl.ANY)
-    moe_out, totals, got_gu, got_down = pl.pallas_call(
+    moe_out, totals, got_gu = pl.pallas_call(
         kernel,
         out_shape=[
             jax.ShapeDtypeStruct((TOK, FEAT), BF),
             jax.ShapeDtypeStruct((8, 128), F32),
             jax.ShapeDtypeStruct(gate_up.shape, BF),
-            jax.ShapeDtypeStruct(down_weight.shape, BF),
         ],
         in_specs=[vmem, vmem, vmem, vmem, hbm, hbm],
-        out_specs=[vmem, vmem, hbm, hbm],
+        out_specs=[vmem, vmem, hbm],
         scratch_shapes=[
             pltpu.VMEM((NZ, TOK + 16, FEAT), BF),
             pltpu.VMEM((4, NZ, MAIN, WIDE), BF),
-            pltpu.VMEM((NE, MAIN, WIDE), BF),
-            pltpu.VMEM((16, UNITS, FEAT), BF),
+            pltpu.VMEM((4 * NE, MAIN, WIDE), BF),
+            pltpu.VMEM((4, UNITS, 4 * FEAT), BF),
             pltpu.VMEM((8 * UNITS, FEAT), BF),
-            pltpu.VMEM((8, TILES, 2 * UNITS, TILE), BF),
             pltpu.VMEM((TILES, 2 * UNITS, TILE), F32),
-            pltpu.VMEM((8, TILES, 2 * UNITS, TILE), BF),
+            pltpu.VMEM((TILES, 2 * UNITS, TILE), F32),
+            pltpu.VMEM((TILES, 2 * UNITS, TILE), F32),
             pltpu.VMEM((TILES, 8, UNITS, TILE), BF),
             pltpu.VMEM((NE * EXT, FEAT), BF),
             pltpu.VMEM((NE, MAIN, WIDE), BF),
@@ -351,8 +388,8 @@
             pltpu.VMEM((8, TOK, FEAT), BF),
             pltpu.VMEM((7, TOK, FEAT), BF),
             pltpu.VMEM((7, TOK, FEAT), BF),
-            pltpu.SemaphoreType.DMA((11,)),
-            pltpu.SemaphoreType.DMA((5,)),
+            pltpu.SemaphoreType.DMA((10,)),
+            pltpu.SemaphoreType.DMA((4,)),
             pltpu.SemaphoreType.DMA((8,)),
             pltpu.SemaphoreType.DMA((7,)),
             pltpu.SemaphoreType.DMA((TILES,)),
@@ -367,6 +404,15 @@
         cost_estimate=pl.CostEstimate(flops=5_000_000_000, bytes_accessed=10_000_000, transcendentals=200_000),
         name="experts",
     )(tokens, expert_ids, route_weight, placement.reshape(1, NE), gate_up, down_weight)
+    got = (got_gu, down_weight)
+    for pair in range(NE // 2):
+        got = lax.cond(
+            swap_flag[pair] == 1,
+            functools.partial(exchange, pair),
+            lambda gu, down, got_gu, got_down: (got_gu, got_down),
+            gate_up, down_weight, *got,
+        )
+    got_gu, got_down = got
     flags = jnp.concatenate([swap_flag, swap_flag]) == 1
     load = totals[0, :NE]
     column_load = jnp.where(flags, jnp.roll(load, NE // 2), load) / jnp.float32(TOK * 8)
@@ -376,7 +422,7 @@
         moe_out,
         column_load,
         jnp.where(swapped, got_gu, gate_up),
-        jnp.where(swapped, got_down, down_weight),
+        got_down,
     )
 
 

time: 388 us -> 309 us (0.80)
  the two profiles are of different devices: /device:TPU:6 before, /device:TPU:190 now
where the time goes in v3:
time: 309 us; the launch traced here: 308 us
  Pallas kernels  276 us (89%)
  between operations  21.8 us (7%)
  local copies, waits for them, and re-layouts  7.98 us (3%)
    pallas_call x1, Pallas kernels, body(): pl.pallas_call(kernel, out_shape=[jax.ShapeDtypeStruct((TOK, FEAT), BF),...  189 us
    pallas_call x12, Pallas kernels, exchange(): pl.pallas_call(functools.partial(exchange_kernel, pair), out_shape=[jax.S...  86.4 us

profile of v3, /device:TPU:190, one launch (start us, length us, event | category | flops | bytes accessed | tf_op | source)
XLA Modules:
  0.0 308.4 jit_solution(1040849944218535495)
XLA Ops:
  0.6 0.8 copy.75.ids
  1.4 0.8 copy.76.weight
  2.2 0.9 copy-done
  3.8 189.3 %experts.1 = (bf16[128,512]{1,0:T(8,128)(2,1)S(1)}, f32[8,128]{1,0:T(8,128)S(1)}, bf16[1,2,96,4096]{3,2,1,0:T(8,128)(2,1)S(1)}) custom-call(bf16[128,512]{1,0:T(8,128)(2,1)S(1)} %copy-done, s32[128,8]{1,0:T(8,128)S(1)} %copy.75.ids, f32[128,8]{1,0:T(8,128)S(1)} %copy.76.weight, s32[1,64]{1,0:T(1,128)S(1)} %bitcast.39, bf16[1,2,96,4096]{3,2,1,0:T(8,128)(2,1)} %gu.1, ...), custom_call_target="tpu_custom_call" | custom-call | flops 5000000000 | bytes 10000000 | tf_op jit(solution)/shard_map/experts/pallas_call | solution.py:365
  215.4 2.6 conditional.32
  215.4 0.9 copy-done.4
  216.3 0.9 copy.78.old_down
  218.0 0.8 conditional.34
  218.0 0.7 exchange.34
  218.7 0.8 conditional.35
  218.8 0.7 exchange.35
  219.6 0.8 conditional.38
  220.3 0.8 conditional.40
  221.1 0.8 conditional.41
  221.9 0.8 conditional.42
  222.7 0.8 conditional.44
  223.5 0.8 conditional.47
  224.4 78.2 %conditional.54 = ((bf16[1,2,96,4096]{3,2,1,0:T(8,128)(2,1)S(1)}, bf16[1,768,512]{2,1,0:T(8,128)(2,1)})) conditional(s32[]{:T(128)} %bitcast.13, (bf16[1,2,96,4096]{3,2,1,0:T(8,128)(2,1)S(1)}, bf16[1,768,512]{2,1,0:T(8,128)(2,1)}) %get-tuple-element.838, (bf16[1,2,96,4096]{3,2,1,0:T(8,128)(2,1)S(1)}, bf16[1,768,512]{2,1,0:T(8,128)(2,1)}, ...), branch_computations={%region_45.0_spmd, %region_46.0_spmd} | conditional | bytes 8 | solution.py:409
  224.4 78.2 %exchange.54 = (bf16[1,2,96,4096]{3,2,1,0:T(8,128)(2,1)S(1)}, bf16[1,768,512]{2,1,0:T(8,128)(2,1)}) custom-call(bf16[1,2,96,4096]{3,2,1,0:T(8,128)(2,1)S(1)} %get-tuple-element.469.gu, bf16[1,768,512]{2,1,0:T(8,128)(2,1)} %get-tuple-element.470.down, ...), custom_call_target="tpu_custom_call", output_to_operand_aliasing={{0}: (2, {}), {1}: (3, {})} | custom-call | tf_op jit(solution)/shard_map/cond/branch_1_fun/exchange/pallas_call | solution.py:349
  302.6 0.8 conditional.59
  302.7 0.7 exchange.59
  303.5 0.8 conditional.62
  305.5 1.3 broadcast_select_fusion
  307.5 0.9 copy.272
  (46 shorter events, 10.2 us)
Async XLA Ops:
  2.2 0.9 copy-start
  3.1 0.7 copy-start.1
  3.8 189.4 %copy-start.6 = (s32[32]{0:T(128)S(1)}, s32[32]{0:T(128)}, u32[]{:S(2)}) copy-start(s32[32]{0:T(128)} %param.75) | copy-start | bytes 388
  3.8 211.6 %copy-start.2 = (bf16[1,2,96,4096]{3,2,1,0:T(8,128)(2,1)S(1)}, bf16[1,2,96,4096]{3,2,1,0:T(8,128)(2,1)}, u32[]{:S(2)}) copy-start(bf16[1,2,96,4096]{3,2,1,0:T(8,128)(2,1)} %gu.1) | copy-start | bytes 4718596
  3.8 211.6 %copy-start.3 = (bf16[1,768,512]{2,1,0:T(8,128)(2,1)S(1)}, bf16[1,768,512]{2,1,0:T(8,128)(2,1)}, u32[]{:S(2)}) copy-start(bf16[1,768,512]{2,1,0:T(8,128)(2,1)} %down.1) | copy-start | bytes 2359300
  215.4 0.9 copy-start.4
  305.5 2.0 copy-start.5

commit v4 on v3

--- a/solution.py
+++ b/solution.py
@@ -69,7 +69,7 @@
 
 def kernel(
     tokens, ids, weight, place, gu, down,
-    out, totals, got_gu,
+    out, totals, got_gu, got_down,
     ring, pick, x_all, w, wd, p_send, p_own, p_in, hid, ext, y_send, y_in, up_out, up_in, dn_out, dn_in,
     snd, rcv, ru, rd, pr, hr, su, sd, loc,
 ):
@@ -132,7 +132,10 @@
     ring[z, TOK:, 0:128] = turned[0:16]
     ring[z, TOK:, 128:256] = turned[16:32]
     ring[z, TOK:, 256:384] = jnp.zeros((16, 128), BF)
-    early = remote(gu.at[0, 0], got_gu.at[0, 0], snd.at[9], rcv.at[3], spouse)
+    early = [
+        remote(gu.at[0, 0, pl.ds(0, 48)], got_gu.at[0, 0, pl.ds(0, 48)], snd.at[9], rcv.at[3], spouse),
+        remote(down.at[0, pl.ds(0, 384)], got_down.at[0, pl.ds(0, 384)], snd.at[10], rcv.at[4], spouse),
+    ]
     ring[z, TOK:, 384:512] = dot(flag(iota((16, TOK), 0) == 0), has.astype(BF)).astype(BF)
 
     pl.semaphore_wait(barrier, len(others))
@@ -206,7 +209,8 @@
     trade.wait_recv()
     await_bytes(x_all.at[pl.ds(0, 15 * NZ)], rcv.at[0])
     await_bytes(x_all.at[pl.ds(0, NZ)], loc.at[2])
-    early.start()
+    for c in early:
+        c.start()
 
     q8 = shuffle8()
 
@@ -321,21 +325,30 @@
     await_bytes(y_in.at[pl.ds(0, 3)], snd.at[6])
     await_bytes(up_out, snd.at[7])
     await_bytes(dn_out, snd.at[8])
-    early.wait()
-
-
-def exchange_kernel(pair, gu, down, old_gu, old_down, got_gu, got_down, snd, rcv):
+    for c in early:
+        c.wait()
+
+
+def exchange_kernel(pairs, gu, down, old_gu, old_down, got_gu, got_down, snd, rcv):
     me = lax.axis_index("expert")
     spouse = {"expert": lax.rem(me + NE // 2, NE)}
 
-    @pl.when(lax.rem(me, NE // 2) == pair)
+    own = lax.rem(me, NE // 2)
+    taking_part = own == pairs[0]
+    for pair in pairs[1:]:
+        taking_part = taking_part | (own == pair)
+
+    @pl.when(taking_part)
     def _():
         barrier = pltpu.get_barrier_semaphore()
         pl.semaphore_signal(barrier, inc=1, device_id=spouse, device_id_type=MESH)
         pl.semaphore_wait(barrier, 1)
+        parts = [(gu, got_gu, (0, 1)), (gu, got_gu, (0, 0, pl.ds(48, 48))), (down, got_down, (0, pl.ds(384, 384)))]
         copies = [
-            pltpu.make_async_remote_copy(src, dst, snd.at[n], rcv.at[n], device_id=spouse, device_id_type=MESH)
-            for n, (src, dst) in enumerate([(gu.at[0, 1], got_gu.at[0, 1]), (down, got_down)])
+            pltpu.make_async_remote_copy(
+                src.at[at], dst.at[at], snd.at[n], rcv.at[n], device_id=spouse, device_id_type=MESH
+            )
+            for n, (src, dst, at) in enumerate(parts)
         ]
         for c in copies:
             c.start()
@@ -343,17 +356,17 @@
             c.wait()
 
 
-def exchange(pair, gu, down, old_gu, old_down):
+def exchange(pairs, number, gu, down, old_gu, old_down):
     hbm = pl.BlockSpec(memory_space=pl.ANY)
     return tuple(
         pl.pallas_call(
-            functools.partial(exchange_kernel, pair),
+            functools.partial(exchange_kernel, pairs),
             out_shape=[jax.ShapeDtypeStruct(old_gu.shape, BF), jax.ShapeDtypeStruct(old_down.shape, BF)],
             in_specs=[hbm] * 4,
             out_specs=[hbm] * 2,
             input_output_aliases={2: 0, 3: 1},
-            scratch_shapes=[pltpu.SemaphoreType.DMA((2,)), pltpu.SemaphoreType.DMA((2,))],
-            compiler_params=pltpu.CompilerParams(collective_id=1 + pair, has_side_effects=True),
+            scratch_shapes=[pltpu.SemaphoreType.DMA((3,)), pltpu.SemaphoreType.DMA((3,))],
+            compiler_params=pltpu.CompilerParams(collective_id=number, has_side_effects=True),
             name="exchange",
         )(gu, down, old_gu, old_down)
     )
@@ -362,15 +375,16 @@
 def body(tokens, expert_ids, route_weight, placement, swap_flag, gate_up, down_weight):
     vmem = pl.BlockSpec(memory_space=pltpu.VMEM)
     hbm = pl.BlockSpec(memory_space=pl.ANY)
-    moe_out, totals, got_gu = pl.pallas_call(
+    moe_out, totals, *got = pl.pallas_call(
         kernel,
         out_shape=[
             jax.ShapeDtypeStruct((TOK, FEAT), BF),
             jax.ShapeDtypeStruct((8, 128), F32),
             jax.ShapeDtypeStruct(gate_up.shape, BF),
+            jax.ShapeDtypeStruct(down_weight.shape, BF),
         ],
         in_specs=[vmem, vmem, vmem, vmem, hbm, hbm],
-        out_specs=[vmem, vmem, hbm],
+        out_specs=[vmem, vmem, hbm, hbm],
         scratch_shapes=[
             pltpu.VMEM((NZ, TOK + 16, FEAT), BF),
             pltpu.VMEM((4, NZ, MAIN, WIDE), BF),
@@ -388,8 +402,8 @@
             pltpu.VMEM((8, TOK, FEAT), BF),
             pltpu.VMEM((7, TOK, FEAT), BF),
             pltpu.VMEM((7, TOK, FEAT), BF),
-            pltpu.SemaphoreType.DMA((10,)),
-            pltpu.SemaphoreType.DMA((4,)),
+            pltpu.SemaphoreType.DMA((11,)),
+            pltpu.SemaphoreType.DMA((5,)),
             pltpu.SemaphoreType.DMA((8,)),
             pltpu.SemaphoreType.DMA((7,)),
             pltpu.SemaphoreType.DMA((TILES,)),
@@ -404,14 +418,13 @@
         cost_estimate=pl.CostEstimate(flops=5_000_000_000, bytes_accessed=10_000_000, transcendentals=200_000),
         name="experts",
     )(tokens, expert_ids, route_weight, placement.reshape(1, NE), gate_up, down_weight)
-    got = (got_gu, down_weight)
-    for pair in range(NE // 2):
-        got = lax.cond(
-            swap_flag[pair] == 1,
-            functools.partial(exchange, pair),
-            lambda gu, down, got_gu, got_down: (got_gu, got_down),
-            gate_up, down_weight, *got,
-        )
+    chosen = jnp.sum(swap_flag.reshape(8, 4) * jnp.array([1, 2, 4, 8], jnp.int32), axis=1)
+    for group in range(8):
+        sets = [lambda gu, down, got_gu, got_down: (got_gu, got_down)]
+        for number in range(1, 16):
+            pairs = tuple(group * 4 + n for n in range(4) if number >> n & 1)
+            sets.append(functools.partial(exchange, pairs, group * 15 + number))
+        got = lax.switch(chosen[group], sets, gate_up, down_weight, *got)
     got_gu, got_down = got
     flags = jnp.concatenate([swap_flag, swap_flag]) == 1
     load = totals[0, :NE]
@@ -422,7 +435,7 @@
         moe_out,
         column_load,
         jnp.where(swapped, got_gu, gate_up),
-        got_down,
+        jnp.where(swapped, got_down, down_weight),
     )
 
 

time: 309 us -> 538 us (1.74)
  the two profiles are of different devices: /device:TPU:190 before, /device:TPU:232 now
where the time goes in v4:
time: 538 us
  Pallas kernels  522 us (97%)
  between operations  6.45 us (1%)
    pallas_call x8, Pallas kernels, exchange(): pl.pallas_call(functools.partial(exchange_kernel, pairs), out_shape=[jax....  335 us
    pallas_call x1, Pallas kernels, body(): pl.pallas_call(kernel, out_shape=[jax.ShapeDtypeStruct((TOK, FEAT), BF),...  186 us

profile of v4, /device:TPU:232, one launch (start us, length us, event | category | flops | bytes accessed | tf_op | source)
XLA Modules:
  0.0 537.8 jit_solution(11127471725302916552)
XLA Ops:
  0.6 0.8 copy.254.ids
  1.4 0.8 copy.255.weight
  2.2 0.9 copy-done
  3.8 186.4 %experts.1 = (bf16[128,512]{1,0:T(8,128)(2,1)S(1)}, f32[8,128]{1,0:T(8,128)S(1)}, bf16[1,2,96,4096]{3,2,1,0:T(8,128)(2,1)S(1)}, bf16[1,768,512]{2,1,0:T(8,128)(2,1)}) custom-call(bf16[128,512]{1,0:T(8,128)(2,1)S(1)} %copy-done, s32[128,8]{1,0:T(8,128)S(1)} %copy.254.ids, f32[128,8]{1,0:T(8,128)S(1)} %copy.255.weight, s32[1,64]{1,0:T(1,128)S(1)} %bitcast.15, ...), custom_call_target="tpu_custom_call" | custom-call | flops 5000000000 | bytes 10000000 | tf_op jit(solution)/shard_map/experts/pallas_call | solution.py:378
  191.1 0.7 fusion.2
  196.8 0.8 conditional.8
  196.9 0.8 exchange.124
  197.6 0.8 conditional.9
  197.7 0.8 exchange.147
  198.5 0.8 conditional.10
  198.5 0.8 exchange.151
  199.3 62.9 %conditional.11 = ((bf16[1,2,96,4096]{3,2,1,0:T(8,128)(2,1)S(1)}, bf16[1,768,512]{2,1,0:T(8,128)(2,1)})) conditional(s32[]{:T(128)} %bitcast.8, (bf16[1,2,96,4096]{3,2,1,0:T(8,128)(2,1)S(1)}, bf16[1,768,512]{2,1,0:T(8,128)(2,1)}) %get-tuple-element.1792, (bf16[1,2,96,4096]{3,2,1,0:T(8,128)(2,1)S(1)}, ...), branch_computations={%region_50.0_spmd, %region_51.0_spmd, %region_52.0_spmd, %region_5... | conditional | bytes 8 | solution.py:427
  199.4 62.9 %exchange.173 = (bf16[1,2,96,4096]{3,2,1,0:T(8,128)(2,1)S(1)}, bf16[1,768,512]{2,1,0:T(8,128)(2,1)}) custom-call(bf16[1,2,96,4096]{3,2,1,0:T(8,128)(2,1)S(1)} %get-tuple-element.1204.gu, bf16[1,768,512]{2,1,0:T(8,128)(2,1)} %get-tuple-element.1205.down, ...), custom_call_target="tpu_custom_call", output_to_operand_aliasing={{0}: (2, {}), {1}: (3, {})} | custom-call | tf_op jit(solution)/shard_map/cond/branch_9_fun/exchange/pallas_call | solution.py:362
  262.3 45.9 %conditional.12 = ((bf16[1,2,96,4096]{3,2,1,0:T(8,128)(2,1)S(1)}, bf16[1,768,512]{2,1,0:T(8,128)(2,1)})) conditional(s32[]{:T(128)} %bitcast.7, (bf16[1,2,96,4096]{3,2,1,0:T(8,128)(2,1)S(1)}, bf16[1,768,512]{2,1,0:T(8,128)(2,1)}) %get-tuple-element.1793, (bf16[1,2,96,4096]{3,2,1,0:T(8,128)(2,1)S(1)}, ...), branch_computations={%region_66.0_spmd, %region_67.0_spmd, %region_68.0_spmd, %region_6... | conditional | bytes 8 | solution.py:427
  262.3 45.8 %exchange.192 = (bf16[1,2,96,4096]{3,2,1,0:T(8,128)(2,1)S(1)}, bf16[1,768,512]{2,1,0:T(8,128)(2,1)}) custom-call(bf16[1,2,96,4096]{3,2,1,0:T(8,128)(2,1)S(1)} %get-tuple-element.1280.gu, bf16[1,768,512]{2,1,0:T(8,128)(2,1)} %get-tuple-element.1281.down, ...), custom_call_target="tpu_custom_call", output_to_operand_aliasing={{0}: (2, {}), {1}: (3, {})} | custom-call | tf_op jit(solution)/shard_map/cond/branch_13_fun/exchange/pallas_call | solution.py:362
  308.1 60.0 %conditional.13 = ((bf16[1,2,96,4096]{3,2,1,0:T(8,128)(2,1)S(1)}, bf16[1,768,512]{2,1,0:T(8,128)(2,1)})) conditional(s32[]{:T(128)} %bitcast.6, (bf16[1,2,96,4096]{3,2,1,0:T(8,128)(2,1)S(1)}, bf16[1,768,512]{2,1,0:T(8,128)(2,1)}) %get-tuple-element.1794, (bf16[1,2,96,4096]{3,2,1,0:T(8,128)(2,1)S(1)}, ...), branch_computations={%region_82.0_spmd, %region_83.0_spmd, %region_84.0_spmd, %region_8... | conditional | bytes 8 | solution.py:427
  308.4 59.8 %exchange.206 = (bf16[1,2,96,4096]{3,2,1,0:T(8,128)(2,1)S(1)}, bf16[1,768,512]{2,1,0:T(8,128)(2,1)}) custom-call(bf16[1,2,96,4096]{3,2,1,0:T(8,128)(2,1)S(1)} %get-tuple-element.1336.gu, bf16[1,768,512]{2,1,0:T(8,128)(2,1)} %get-tuple-element.1337.down, ...), custom_call_target="tpu_custom_call", output_to_operand_aliasing={{0}: (2, {}), {1}: (3, {})} | custom-call | tf_op jit(solution)/shard_map/cond/branch_12_fun/exchange/pallas_call | solution.py:362
  368.2 59.2 %conditional.14 = ((bf16[1,2,96,4096]{3,2,1,0:T(8,128)(2,1)S(1)}, bf16[1,768,512]{2,1,0:T(8,128)(2,1)})) conditional(s32[]{:T(128)} %bitcast.5, (bf16[1,2,96,4096]{3,2,1,0:T(8,128)(2,1)S(1)}, bf16[1,768,512]{2,1,0:T(8,128)(2,1)}) %get-tuple-element.1795, (bf16[1,2,96,4096]{3,2,1,0:T(8,128)(2,1)S(1)}, ...), branch_computations={%region_98.0_spmd, %region_99.0_spmd, %region_100.0_spmd, %region_... | conditional | bytes 8 | solution.py:427
  368.2 59.2 %exchange.216 = (bf16[1,2,96,4096]{3,2,1,0:T(8,128)(2,1)S(1)}, bf16[1,768,512]{2,1,0:T(8,128)(2,1)}) custom-call(bf16[1,2,96,4096]{3,2,1,0:T(8,128)(2,1)S(1)} %get-tuple-element.1376.gu, bf16[1,768,512]{2,1,0:T(8,128)(2,1)} %get-tuple-element.1377.down, ...), custom_call_target="tpu_custom_call", output_to_operand_aliasing={{0}: (2, {}), {1}: (3, {})} | custom-call | tf_op jit(solution)/shard_map/cond/branch_7_fun/exchange/pallas_call | solution.py:362
  427.4 105.5 %conditional.15 = ((bf16[1,2,96,4096]{3,2,1,0:T(8,128)(2,1)S(1)}, bf16[1,768,512]{2,1,0:T(8,128)(2,1)})) conditional(s32[]{:T(128)} %bitcast.4, (bf16[1,2,96,4096]{3,2,1,0:T(8,128)(2,1)S(1)}, bf16[1,768,512]{2,1,0:T(8,128)(2,1)}) %get-tuple-element.1796, (bf16[1,2,96,4096]{3,2,1,0:T(8,128)(2,1)S(1)}, ...), branch_computations={%region_114.0_spmd, %region_115.0_spmd, %region_116.0_spmd, %regio... | conditional | bytes 8 | solution.py:427
  427.5 105.5 %exchange.236 = (bf16[1,2,96,4096]{3,2,1,0:T(8,128)(2,1)S(1)}, bf16[1,768,512]{2,1,0:T(8,128)(2,1)}) custom-call(bf16[1,2,96,4096]{3,2,1,0:T(8,128)(2,1)S(1)} %get-tuple-element.1456.gu, bf16[1,768,512]{2,1,0:T(8,128)(2,1)} %get-tuple-element.1457.down, ...), custom_call_target="tpu_custom_call", output_to_operand_aliasing={{0}: (2, {}), {1}: (3, {})} | custom-call | tf_op jit(solution)/shard_map/cond/branch_12_fun/exchange/pallas_call | solution.py:362
  534.3 1.3 broadcast_select_fusion
  536.2 1.0 broadcast_select_fusion.1
  537.1 0.7 copy.753
  (20 shorter events, 2.8 us)
Async XLA Ops:
  2.2 0.9 copy-start
  3.1 0.7 copy-start.1
  3.8 186.5 %copy-start.5 = (s32[32]{0:T(128)S(1)}, s32[32]{0:T(128)}, u32[]{:S(2)}) copy-start(s32[32]{0:T(128)} %param.140) | copy-start | bytes 388
  3.8 187.2 %copy-start.7 = (s32[4]{0:T(128)S(1)}, s32[4]{0:T(128)}, u32[]{:S(2)}) copy-start(s32[4]{0:T(128)} %constant.45.clone) | copy-start | bytes 52
  3.8 193.0 %copy-start.2 = (bf16[1,2,96,4096]{3,2,1,0:T(8,128)(2,1)S(1)}, bf16[1,2,96,4096]{3,2,1,0:T(8,128)(2,1)}, u32[]{:S(2)}) copy-start(bf16[1,2,96,4096]{3,2,1,0:T(8,128)(2,1)} %gu.1) | copy-start | bytes 4718596
  427.4 105.6 %copy-start.6 = (s32[32]{0:T(128)S(1)}, s32[32]{0:T(128)}, u32[]{:S(2)}) copy-start(s32[32]{0:T(128)} %param.140) | copy-start | bytes 388
  534.2 1.3 copy-start.3
  534.3 1.9 copy-start.4

commit v5 on v4

--- a/solution.py
+++ b/solution.py
@@ -329,16 +329,11 @@
         c.wait()
 
 
-def exchange_kernel(pairs, gu, down, old_gu, old_down, got_gu, got_down, snd, rcv):
+def exchange_kernel(pair, gu, down, old_gu, old_down, got_gu, got_down, snd, rcv):
     me = lax.axis_index("expert")
     spouse = {"expert": lax.rem(me + NE // 2, NE)}
 
-    own = lax.rem(me, NE // 2)
-    taking_part = own == pairs[0]
-    for pair in pairs[1:]:
-        taking_part = taking_part | (own == pair)
-
-    @pl.when(taking_part)
+    @pl.when(lax.rem(me, NE // 2) == pair)
     def _():
         barrier = pltpu.get_barrier_semaphore()
         pl.semaphore_signal(barrier, inc=1, device_id=spouse, device_id_type=MESH)
@@ -356,17 +351,17 @@
             c.wait()
 
 
-def exchange(pairs, number, gu, down, old_gu, old_down):
+def exchange(pair, gu, down, old_gu, old_down):
     hbm = pl.BlockSpec(memory_space=pl.ANY)
     return tuple(
         pl.pallas_call(
-            functools.partial(exchange_kernel, pairs),
+            functools.partial(exchange_kernel, pair),
             out_shape=[jax.ShapeDtypeStruct(old_gu.shape, BF), jax.ShapeDtypeStruct(old_down.shape, BF)],
             in_specs=[hbm] * 4,
             out_specs=[hbm] * 2,
             input_output_aliases={2: 0, 3: 1},
             scratch_shapes=[pltpu.SemaphoreType.DMA((3,)), pltpu.SemaphoreType.DMA((3,))],
-            compiler_params=pltpu.CompilerParams(collective_id=number, has_side_effects=True),
+            compiler_params=pltpu.CompilerParams(collective_id=1 + pair, has_side_effects=True),
             name="exchange",
         )(gu, down, old_gu, old_down)
     )
@@ -418,13 +413,15 @@
         cost_estimate=pl.CostEstimate(flops=5_000_000_000, bytes_accessed=10_000_000, transcendentals=200_000),
         name="experts",
     )(tokens, expert_ids, route_weight, placement.reshape(1, NE), gate_up, down_weight)
-    chosen = jnp.sum(swap_flag.reshape(8, 4) * jnp.array([1, 2, 4, 8], jnp.int32), axis=1)
-    for group in range(8):
-        sets = [lambda gu, down, got_gu, got_down: (got_gu, got_down)]
-        for number in range(1, 16):
-            pairs = tuple(group * 4 + n for n in range(4) if number >> n & 1)
-            sets.append(functools.partial(exchange, pairs, group * 15 + number))
-        got = lax.switch(chosen[group], sets, gate_up, down_weight, *got)
+    word = jnp.sum(swap_flag[: NE // 2] << jnp.arange(NE // 2, dtype=jnp.int32))
+    word = lax.optimization_barrier(word)
+    for pair in range(NE // 2):
+        got = lax.cond(
+            (word >> pair) & 1 == 1,
+            functools.partial(exchange, pair),
+            lambda gu, down, got_gu, got_down: (got_gu, got_down),
+            gate_up, down_weight, *got,
+        )
     got_gu, got_down = got
     flags = jnp.concatenate([swap_flag, swap_flag]) == 1
     load = totals[0, :NE]

time: 538 us -> 327 us (0.61)
  the two profiles are of different devices: /device:TPU:232 before, /device:TPU:109 now
where the time goes in v5:
time: 327 us; the launch traced here: 326 us
  Pallas kernels  295 us (90%)
  between operations  22.3 us (7%)
  local copies, waits for them, and re-layouts  4.48 us (1%)
  other arithmetic  4.16 us (1%)
    pallas_call x1, Pallas kernels, body(): pl.pallas_call(kernel, out_shape=[jax.ShapeDtypeStruct((TOK, FEAT), BF),...  187 us
    pallas_call x19, Pallas kernels, exchange(): pl.pallas_call(functools.partial(exchange_kernel, pair), out_shape=[jax.S...  108 us

profile of v5, /device:TPU:109, one launch (start us, length us, event | category | flops | bytes accessed | tf_op | source)
XLA Modules:
  0.0 326.4 jit_solution(7605668567969444558)
XLA Ops:
  0.6 1.3 fusion.1
  2.6 0.8 copy.75.ids
  3.4 0.8 copy.76.weight
  4.2 0.9 copy-done
  5.7 187.3 %experts.1 = (bf16[128,512]{1,0:T(8,128)(2,1)S(1)}, f32[8,128]{1,0:T(8,128)S(1)}, bf16[1,2,96,4096]{3,2,1,0:T(8,128)(2,1)S(1)}, bf16[1,768,512]{2,1,0:T(8,128)(2,1)}) custom-call(bf16[128,512]{1,0:T(8,128)(2,1)S(1)} %copy-done, s32[128,8]{1,0:T(8,128)S(1)} %copy.75.ids, f32[128,8]{1,0:T(8,128)S(1)} %copy.76.weight, s32[1,64]{1,0:T(1,128)S(1)} %bitcast.7, ...), custom_call_target="tpu_custom_call" | custom-call | flops 5000000000 | bytes 10000000 | tf_op jit(solution)/shard_map/experts/pallas_call | solution.py:373
  193.1 0.8 conditional.32
  194.5 0.8 conditional.33
  197.9 0.8 conditional.37
  199.4 0.8 conditional.38
  200.8 0.8 conditional.39
  202.2 0.8 conditional.40
  203.7 0.8 conditional.41
  206.4 0.8 conditional.44
  209.2 94.0 %conditional.47 = ((bf16[1,2,96,4096]{3,2,1,0:T(8,128)(2,1)S(1)}, bf16[1,768,512]{2,1,0:T(8,128)(2,1)})) conditional(s32[]{:T(128)} %convert_element_type.112, (bf16[1,2,96,4096]{3,2,1,0:T(8,128)(2,1)S(1)}, bf16[1,768,512]{2,1,0:T(8,128)(2,1)}) %get-tuple-element.806, (bf16[1,2,96,4096]{3,2,1,0:T(8,128)(2,1)S(1)}, bf16[1,768,512]{2,1,0:T(8,128)(2,1)}, ...), branch_computations={%region_32.0_spmd, %region_33.0_spmd} | conditional | bytes 8 | solution.py:419
  209.2 94.0 %exchange.47 = (bf16[1,2,96,4096]{3,2,1,0:T(8,128)(2,1)S(1)}, bf16[1,768,512]{2,1,0:T(8,128)(2,1)}) custom-call(bf16[1,2,96,4096]{3,2,1,0:T(8,128)(2,1)S(1)} %get-tuple-element.444.gu, bf16[1,768,512]{2,1,0:T(8,128)(2,1)} %get-tuple-element.445.down, ...), custom_call_target="tpu_custom_call", output_to_operand_aliasing={{0}: (2, {}), {1}: (3, {})} | custom-call | tf_op jit(solution)/shard_map/cond/branch_1_fun/exchange/pallas_call | solution.py:357
  305.2 0.8 conditional.50
  306.6 0.8 conditional.51
  308.7 0.8 conditional.53
  310.2 0.8 conditional.54
  311.6 0.8 conditional.55
  318.0 0.8 conditional.60
  319.4 0.8 conditional.61
  322.2 1.3 broadcast_select_fusion
  324.1 1.0 broadcast_select_fusion.1
  (48 shorter events, 18.7 us)
Async XLA Ops:
  4.2 0.9 copy-start
  5.1 0.7 copy-start.1
  5.7 187.3 %copy-start.2 = (bf16[1,2,96,4096]{3,2,1,0:T(8,128)(2,1)S(1)}, bf16[1,2,96,4096]{3,2,1,0:T(8,128)(2,1)}, u32[]{:S(2)}) copy-start(bf16[1,2,96,4096]{3,2,1,0:T(8,128)(2,1)} %gu.1) | copy-start | bytes 4718596
  322.2 1.3 copy-start.3
  322.2 1.9 copy-start.4
  323.5 1.6 copy-start.5

commit v6 on v5

--- a/solution.py
+++ b/solution.py
@@ -140,15 +140,18 @@
 
     pl.semaphore_wait(barrier, len(others))
 
-    def pass_up(block, s):
-        remote(ring.at[block], ring.at[block], snd.at[0], ru.at[s], above).start()
-
-    def pass_down(block, s):
-        remote(ring.at[block], ring.at[block], snd.at[1], rd.at[s], below).start()
-
-    pass_up(z, 0)
-    pass_down(z, 0)
-
+    def part_of(block, h):
+        return ring.at[block, pl.ds(80 * h, 80 - 16 * h)]
+
+    def pass_up(block, s, h):
+        remote(part_of(block, h), part_of(block, h), snd.at[0], ru.at[2 * s + h], above).start()
+
+    def pass_down(block, s, h):
+        remote(part_of(block, h), part_of(block, h), snd.at[1], rd.at[2 * s + h], below).start()
+
+    for h in range(2):
+        pass_up(z, 0, h)
+        pass_down(z, 0, h)
     trade = remote(gu.at[0, :, :, other_half], w.at[pl.ds(2, 2)], snd.at[3], rcv.at[1], across)
     trade.start()
 
@@ -185,13 +188,14 @@
 
     def around(s, carry):
         low, high = lax.rem(z + 15 - s, NZ), lax.rem(z + 1 + s, NZ)
-        await_bytes(ring.at[low], ru.at[s])
-        pass_up(low, s + 1)
-        await_bytes(ring.at[high], rd.at[s])
-
-        @pl.when(s < 6)
-        def _():
-            pass_down(high, s + 1)
+        for h in range(2):
+            await_bytes(part_of(low, h), ru.at[2 * s + h])
+            pass_up(low, s + 1, h)
+            await_bytes(part_of(high, h), rd.at[2 * s + h])
+
+            @pl.when(s < 6)
+            def _(h=h):
+                pass_down(high, s + 1, h)
 
         choose(low, 2 * s + 1)
         choose(high, 2 * s + 2)
@@ -200,7 +204,10 @@
 
     lax.fori_loop(0, 7, around, 0)
     far = lax.rem(z + 8, NZ)
-    await_bytes(ring.at[far], ru.at[7])
+    for h in range(2):
+        await_bytes(part_of(far, h), ru.at[14 + h])
+    for c in early:
+        c.start()
     choose(far, 15)
     deal(15, 1)
 
@@ -209,8 +216,6 @@
     trade.wait_recv()
     await_bytes(x_all.at[pl.ds(0, 15 * NZ)], rcv.at[0])
     await_bytes(x_all.at[pl.ds(0, NZ)], loc.at[2])
-    for c in early:
-        c.start()
 
     q8 = shuffle8()
 
@@ -286,35 +291,39 @@
             share = share + dot(mix.astype(BF), rows, TN)
         return share
 
-    def hand_up(s, total):
-        up_out[s] = total.astype(BF)
-        remote(up_out.at[s], up_in.at[s], snd.at[7], su.at[s], above).start()
-
-    def hand_down(s, total):
-        dn_out[s] = total.astype(BF)
-        remote(dn_out.at[s], dn_in.at[s], snd.at[8], sd.at[s], below).start()
-
-    hand_up(0, combine(far, 15))
-    hand_down(0, combine(lax.rem(z + 9, NZ), 13))
+    def hand(s, share, come, go, sem, sent, device, first=False):
+        for h in range(2):
+            rows = pl.ds(64 * h, 64)
+            total = share[64 * h : 64 * h + 64]
+            if not first:
+                await_bytes(come.at[s - 1, rows], sem.at[2 * s - 2 + h])
+                total = total + come[s - 1, rows, :].astype(F32)
+            go[s, rows, :] = total.astype(BF)
+            remote(go.at[s, rows], come.at[s, rows], sent, sem.at[2 * s + h], device).start()
+
+    def hand_up(s, share, first=False):
+        hand(s, share, up_in, up_out, su, snd.at[7], above, first)
+
+    def hand_down(s, share, first=False):
+        hand(s, share, dn_in, dn_out, sd, snd.at[8], below, first)
+
+    hand_up(0, combine(far, 15), True)
+    hand_down(0, combine(lax.rem(z + 9, NZ), 13), True)
 
     def home(s, carry):
-        share = combine(lax.rem(z + 8 - s, NZ), 16 - 2 * s)
-        await_bytes(up_in.at[s - 1], su.at[s - 1])
-        hand_up(s, share + up_in[s - 1].astype(F32))
-        share = combine(lax.rem(z + 9 + s, NZ), 13 - 2 * s)
-        await_bytes(dn_in.at[s - 1], sd.at[s - 1])
-        hand_down(s, share + dn_in[s - 1].astype(F32))
+        hand_up(s, combine(lax.rem(z + 8 - s, NZ), 16 - 2 * s))
+        hand_down(s, combine(lax.rem(z + 9 + s, NZ), 13 - 2 * s))
         return carry
 
     lax.fori_loop(1, 7, home, 0)
-    share = combine(lax.rem(z + 1, NZ), 2)
-    await_bytes(up_in.at[6], su.at[6])
-    hand_up(7, share + up_in[6].astype(F32))
+    hand_up(7, combine(lax.rem(z + 1, NZ), 2))
     share = combine(z, 0)
-    await_bytes(dn_in.at[6], sd.at[6])
-    share = share + dn_in[6].astype(F32)
-    await_bytes(up_in.at[7], su.at[7])
-    out[...] = (share + up_in[7].astype(F32)).astype(BF)
+    for h in range(2):
+        rows = pl.ds(64 * h, 64)
+        await_bytes(dn_in.at[6, rows], sd.at[12 + h])
+        total = share[64 * h : 64 * h + 64] + dn_in[6, rows, :].astype(F32)
+        await_bytes(up_in.at[7, rows], su.at[14 + h])
+        out[rows, :] = (total + up_in[7, rows, :].astype(F32)).astype(BF)
 
     await_bytes(ring.at[pl.ds(0, 8)], snd.at[0])
     await_bytes(ring.at[pl.ds(0, 7)], snd.at[1])
@@ -399,12 +408,12 @@
             pltpu.VMEM((7, TOK, FEAT), BF),
             pltpu.SemaphoreType.DMA((11,)),
             pltpu.SemaphoreType.DMA((5,)),
-            pltpu.SemaphoreType.DMA((8,)),
-            pltpu.SemaphoreType.DMA((7,)),
+            pltpu.SemaphoreType.DMA((16,)),
+            pltpu.SemaphoreType.DMA((14,)),
             pltpu.SemaphoreType.DMA((TILES,)),
             pltpu.SemaphoreType.DMA((TILES,)),
-            pltpu.SemaphoreType.DMA((8,)),
-            pltpu.SemaphoreType.DMA((7,)),
+            pltpu.SemaphoreType.DMA((16,)),
+            pltpu.SemaphoreType.DMA((14,)),
             pltpu.SemaphoreType.DMA((4,)),
         ],
         compiler_params=pltpu.CompilerParams(

time: 327 us -> 326 us (level)
  the two profiles are of different devices: /device:TPU:109 before, /device:TPU:192 now
where the time goes in v6:
time: 326 us; the launch traced here: 325 us
  Pallas kernels  293 us (90%)
  between operations  22.3 us (7%)
  local copies, waits for them, and re-layouts  4.48 us (1%)
  other arithmetic  4.16 us (1%)
    pallas_call x1, Pallas kernels, body(): pl.pallas_call(kernel, out_shape=[jax.ShapeDtypeStruct((TOK, FEAT), BF),...  200 us
    pallas_call x17, Pallas kernels, exchange(): pl.pallas_call(functools.partial(exchange_kernel, pair), out_shape=[jax.S...  93.6 us

profile of v6, /device:TPU:192, one launch (start us, length us, event | category | flops | bytes accessed | tf_op | source)
XLA Modules:
  0.0 324.6 jit_solution(13351604477151319901)
XLA Ops:
  0.6 1.3 fusion.1
  2.6 0.8 copy.75.ids
  3.4 0.8 copy.76.weight
  4.2 0.9 copy-done
  5.7 199.7 %experts.1 = (bf16[128,512]{1,0:T(8,128)(2,1)S(1)}, f32[8,128]{1,0:T(8,128)S(1)}, bf16[1,2,96,4096]{3,2,1,0:T(8,128)(2,1)S(1)}, bf16[1,768,512]{2,1,0:T(8,128)(2,1)}) custom-call(bf16[128,512]{1,0:T(8,128)(2,1)S(1)} %copy-done, s32[128,8]{1,0:T(8,128)S(1)} %copy.75.ids, f32[128,8]{1,0:T(8,128)S(1)} %copy.76.weight, s32[1,64]{1,0:T(1,128)S(1)} %bitcast.7, ...), custom_call_target="tpu_custom_call" | custom-call | flops 5000000000 | bytes 10000000 | tf_op jit(solution)/shard_map/experts/pallas_call | solution.py:382
  208.7 0.8 conditional.37
  211.5 0.8 conditional.40
  212.9 0.8 conditional.41
  215.0 0.8 conditional.43
  216.4 0.8 conditional.44
  217.9 0.8 conditional.45
  220.0 0.8 conditional.47
  222.1 0.8 conditional.49
  223.5 0.8 conditional.50
  224.9 0.8 conditional.51
  227.7 0.8 conditional.54
  229.8 81.4 %conditional.56 = ((bf16[1,2,96,4096]{3,2,1,0:T(8,128)(2,1)S(1)}, bf16[1,768,512]{2,1,0:T(8,128)(2,1)})) conditional(s32[]{:T(128)} %convert_element_type.103, (bf16[1,2,96,4096]{3,2,1,0:T(8,128)(2,1)S(1)}, bf16[1,768,512]{2,1,0:T(8,128)(2,1)}) %get-tuple-element.815, (bf16[1,2,96,4096]{3,2,1,0:T(8,128)(2,1)S(1)}, bf16[1,768,512]{2,1,0:T(8,128)(2,1)}, ...), branch_computations={%region_50.0_spmd, %region_51.0_spmd} | conditional | bytes 8 | solution.py:428
  229.8 81.4 %exchange.56 = (bf16[1,2,96,4096]{3,2,1,0:T(8,128)(2,1)S(1)}, bf16[1,768,512]{2,1,0:T(8,128)(2,1)}) custom-call(bf16[1,2,96,4096]{3,2,1,0:T(8,128)(2,1)S(1)} %get-tuple-element.480.gu, bf16[1,768,512]{2,1,0:T(8,128)(2,1)} %get-tuple-element.481.down, ...), custom_call_target="tpu_custom_call", output_to_operand_aliasing={{0}: (2, {}), {1}: (3, {})} | custom-call | tf_op jit(solution)/shard_map/cond/branch_1_fun/exchange/pallas_call | solution.py:366
  311.9 0.8 conditional.57
  313.3 0.8 conditional.58
  315.4 0.8 conditional.60
  316.8 0.8 conditional.61
  320.4 1.3 broadcast_select_fusion
  322.3 1.0 broadcast_select_fusion.1
  (46 shorter events, 15.7 us)
Async XLA Ops:
  4.2 0.9 copy-start
  5.1 0.7 copy-start.1
  5.7 199.7 %copy-start.2 = (bf16[1,2,96,4096]{3,2,1,0:T(8,128)(2,1)S(1)}, bf16[1,2,96,4096]{3,2,1,0:T(8,128)(2,1)}, u32[]{:S(2)}) copy-start(bf16[1,2,96,4096]{3,2,1,0:T(8,128)(2,1)} %gu.1) | copy-start | bytes 4718596
  320.3 1.3 copy-start.3
  320.4 1.9 copy-start.4
  321.7 1.6 copy-start.5

commit v7 on v6

--- a/solution.py
+++ b/solution.py
@@ -206,8 +206,6 @@
     far = lax.rem(z + 8, NZ)
     for h in range(2):
         await_bytes(part_of(far, h), ru.at[14 + h])
-    for c in early:
-        c.start()
     choose(far, 15)
     deal(15, 1)
 
@@ -216,6 +214,8 @@
     trade.wait_recv()
     await_bytes(x_all.at[pl.ds(0, 15 * NZ)], rcv.at[0])
     await_bytes(x_all.at[pl.ds(0, NZ)], loc.at[2])
+    for c in early:
+        c.start()
 
     q8 = shuffle8()
 

time: 326 us -> 324 us (level)
    pallas_call x1, Pallas kernels: 200 us -> 186 us  [body(): pl.pallas_call(kernel, out_shape=[jax.ShapeDtypeStruct((TOK, FEAT), BF),...]
    pallas_call x17 -> x22, Pallas kernels: 93.6 us -> 104 us  [exchange(): pl.pallas_call(functools.partial(exchange_kernel, pair), out_shape=[jax.S...]
where the time goes in v7:
time: 324 us; the launch traced here: 321 us
  Pallas kernels  290 us (90%)
  between operations  22.3 us (7%)
  local copies, waits for them, and re-layouts  4.48 us (1%)
  other arithmetic  4.16 us (1%)
    pallas_call x1, Pallas kernels, body(): pl.pallas_call(kernel, out_shape=[jax.ShapeDtypeStruct((TOK, FEAT), BF),...  186 us
    pallas_call x22, Pallas kernels, exchange(): pl.pallas_call(functools.partial(exchange_kernel, pair), out_shape=[jax.S...  104 us

profile of v7, /device:TPU:192, one launch (start us, length us, event | category | flops | bytes accessed | tf_op | source)
XLA Modules:
  0.0 321.5 jit_solution(14437524922699763829)
XLA Ops:
  0.6 1.3 fusion.1
  2.6 0.8 copy.75.ids
  3.4 0.8 copy.76.weight
  4.2 0.9 copy-done
  5.7 185.7 %experts.1 = (bf16[128,512]{1,0:T(8,128)(2,1)S(1)}, f32[8,128]{1,0:T(8,128)S(1)}, bf16[1,2,96,4096]{3,2,1,0:T(8,128)(2,1)S(1)}, bf16[1,768,512]{2,1,0:T(8,128)(2,1)}) custom-call(bf16[128,512]{1,0:T(8,128)(2,1)S(1)} %copy-done, s32[128,8]{1,0:T(8,128)S(1)} %copy.75.ids, f32[128,8]{1,0:T(8,128)S(1)} %copy.76.weight, s32[1,64]{1,0:T(1,128)S(1)} %bitcast.7, ...), custom_call_target="tpu_custom_call" | custom-call | flops 5000000000 | bytes 10000000 | tf_op jit(solution)/shard_map/experts/pallas_call | solution.py:382
  191.4 0.8 conditional.32
  194.2 0.8 conditional.35
  195.6 0.8 conditional.36
  197.0 0.8 conditional.37
  198.5 0.8 conditional.38
  200.6 0.8 conditional.40
  202.7 0.8 conditional.42
  204.1 0.8 conditional.43
  205.5 0.8 conditional.44
  213.4 0.8 conditional.50
  219.0 0.8 conditional.55
  220.4 88.5 %conditional.56 = ((bf16[1,2,96,4096]{3,2,1,0:T(8,128)(2,1)S(1)}, bf16[1,768,512]{2,1,0:T(8,128)(2,1)})) conditional(s32[]{:T(128)} %convert_element_type.103, (bf16[1,2,96,4096]{3,2,1,0:T(8,128)(2,1)S(1)}, bf16[1,768,512]{2,1,0:T(8,128)(2,1)}) %get-tuple-element.815, (bf16[1,2,96,4096]{3,2,1,0:T(8,128)(2,1)S(1)}, bf16[1,768,512]{2,1,0:T(8,128)(2,1)}, ...), branch_computations={%region_50.0_spmd, %region_51.0_spmd} | conditional | bytes 8 | solution.py:428
  220.4 88.5 %exchange.56 = (bf16[1,2,96,4096]{3,2,1,0:T(8,128)(2,1)S(1)}, bf16[1,768,512]{2,1,0:T(8,128)(2,1)}) custom-call(bf16[1,2,96,4096]{3,2,1,0:T(8,128)(2,1)S(1)} %get-tuple-element.480.gu, bf16[1,768,512]{2,1,0:T(8,128)(2,1)} %get-tuple-element.481.down, ...), custom_call_target="tpu_custom_call", output_to_operand_aliasing={{0}: (2, {}), {1}: (3, {})} | custom-call | tf_op jit(solution)/shard_map/cond/branch_1_fun/exchange/pallas_call | solution.py:366
  309.5 0.8 conditional.57
  311.6 0.8 conditional.59
  313.1 0.8 conditional.60
  315.2 0.8 conditional.62
  317.3 1.3 broadcast_select_fusion
  319.2 1.0 broadcast_select_fusion.1
  (51 shorter events, 23.3 us)
Async XLA Ops:
  4.2 0.9 copy-start
  5.1 0.7 copy-start.1
  5.7 185.7 %copy-start.2 = (bf16[1,2,96,4096]{3,2,1,0:T(8,128)(2,1)S(1)}, bf16[1,2,96,4096]{3,2,1,0:T(8,128)(2,1)}, u32[]{:S(2)}) copy-start(bf16[1,2,96,4096]{3,2,1,0:T(8,128)(2,1)} %gu.1) | copy-start | bytes 4718596
  317.2 1.3 copy-start.3
  317.3 1.9 copy-start.4
  318.6 1.6 copy-start.5
